TPU v7x, 128 devices: a whole 4x4x4 slice. The times are simulated.
128 devices in a mesh: fsdp: 4 (over y), dp: 16 (over z_lo, x, core), owner: 2 (over z_hi).
Axes of the slice: x: 4, y: 4, z: 4 (z_hi: 2, z_lo: 2; z = z_hi * 2 + z_lo), core: 2. Of those that a mesh axis runs over, the one named last changes fastest.
Arguments:
- tokens: bfloat16 [65536, 4608], P(('fsdp', 'dp', 'owner')), may hold values from -6 to 6
- output_gradient: bfloat16 [65536, 2048], P(('fsdp', 'dp', 'owner')), may hold values from -6 to 6
- tile_language: int32 [512], replicated, may hold values from 0 to 63, as said below
- tile_live_count: int32 [512], replicated, may hold values from 1 to 128, as said below
- frozen_weight: bfloat16 [4608, 2048], P('fsdp'), may hold values from -0.09375 to 0.09375
- adapter_down: bfloat16 [64, 32, 4608], P('owner', None, 'fsdp'), may hold values from -0.09375 to 0.09375
- adapter_up: bfloat16 [64, 32, 2048], P('owner', None, 'fsdp'), may hold values from -1 to 1
Outputs:
- input_gradient: bfloat16 [65536, 4608], P(('fsdp', 'dp', 'owner'))
- grad_down: bfloat16 [64, 32, 4608], P('owner', None, 'fsdp')
- grad_up: bfloat16 [64, 32, 2048], P('owner', None, 'fsdp')
Inputs may be any that keep to these rules, and one draw needn't show every extreme that they name: `tile_language`: the tiles of the device with fsdp index f, dp index e and owner index o are tiles ((f * 16 + e) * 2 + o) * 4 onward; all of them name languages o * 32 to (o + 1) * 32 - 1. `tile_live_count`: the live slots of a tile are its first ones.
All inputs are finite; a program needn't handle non-finite values.
Results may differ from a plain program's by a relative error of at most 0.0051.
Values may be sent and summed in bfloat16 or wider, within the bound.
A program may use at most 128 MiB of HBM per device.

v0:
```python
import jax
import jax.numpy as jnp
from jax import lax
from jax.sharding import PartitionSpec as P

TILE_TOKENS = 128


adapter_scale = 2.0


def tiled_input(array, size):
    return array.reshape(array.shape[0] // size, size, array.shape[1])


def combine_tiles(local_lang, lang_count, partial_value):
    onehot = (local_lang[None, :] == jnp.arange(lang_count, dtype=jnp.int32)[:, None]).astype(
        jnp.float32
    )
    return jnp.einsum("jk,krd->jrd", onehot, partial_value, precision=lax.Precision.HIGHEST)


def on_device(
    tokens, output_gradient, tile_language, tile_live_count, frozen_weight, adapter_down, adapter_up
):
    fsdp_count = lax.axis_size("fsdp")
    dp_count = lax.axis_size("dp")
    owner_count = lax.axis_size("owner")
    fsdp_rank = lax.axis_index("fsdp")
    dp_rank = lax.axis_index("dp")
    owner_rank = lax.axis_index("owner")
    tok_rows, width = tokens.shape
    tiles_dev = tok_rows // TILE_TOKENS
    language_owner = adapter_down.shape[0]
    device = (fsdp_rank * dp_count + dp_rank) * owner_count + owner_rank
    offsets = jnp.arange(tiles_dev, dtype=jnp.int32)
    sources = jnp.arange(fsdp_count, dtype=jnp.int32)
    slots = jnp.arange(TILE_TOKENS, dtype=jnp.int32)
    group_ids = (
        ((sources[:, None] * dp_count + dp_rank) * owner_count + owner_rank) * tiles_dev
        + offsets[None, :]
    ).reshape(-1)
    group_lang = jnp.take(tile_language, group_ids) - owner_rank * language_owner
    own_ids = device * tiles_dev + offsets
    own_lang = jnp.take(tile_language, own_ids) - owner_rank * language_owner
    owned_live_mask = (slots[None, :] < jnp.take(tile_live_count, own_ids)[:, None])[:, :, None]
    every_tile = tok_rows * fsdp_count * dp_count * owner_count
    adapter_factor = adapter_scale * float(every_tile) ** (-0.5)
    down_full, up_full = (
        lax.all_gather(adapter_down, "fsdp", axis=2, tiled=True),
        lax.all_gather(adapter_up, "fsdp", axis=2, tiled=True),
    )
    selected_down = jnp.take(down_full, own_lang, axis=0)
    selected_up = jnp.take(up_full, own_lang, axis=0)
    tok_tiles = tiled_input(tokens, TILE_TOKENS)
    gradient_tiles = tiled_input(output_gradient, TILE_TOKENS)
    hidden_state = jnp.where(
        owned_live_mask,
        jnp.einsum("ktd,krd->ktr", tok_tiles, selected_down, preferred_element_type=jnp.float32),
        0.0,
    ).astype(jnp.bfloat16)
    backward_input = jnp.where(
        owned_live_mask,
        jnp.einsum("bca,bea->bce", gradient_tiles, selected_up, preferred_element_type=jnp.float32),
        0.0,
    ).astype(jnp.bfloat16)
    frozen_output = jnp.dot(
        output_gradient,
        lax.all_gather(frozen_weight, "fsdp", axis=0, tiled=True).T,
        preferred_element_type=jnp.float32,
    )
    adapter_extra = jnp.einsum(
        "ktr,krd->ktd", backward_input, selected_down, preferred_element_type=jnp.float32
    )
    input_gradient = (
        jnp.where(
            owned_live_mask,
            tiled_input(frozen_output, TILE_TOKENS) + adapter_scale * adapter_extra,
            0.0,
        )
        .astype(jnp.bfloat16)
        .reshape(tok_rows, width)
    )
    part_down = jnp.einsum(
        "ktr,ktd->krd", backward_input, tok_tiles, preferred_element_type=jnp.float32
    )
    partial_up = jnp.einsum(
        "sow,soz->swz", hidden_state, gradient_tiles, preferred_element_type=jnp.float32
    )
    part_down, partial_up = (
        lax.all_to_all(part_down, "fsdp", split_axis=2, concat_axis=0, tiled=True),
        lax.all_to_all(partial_up, "fsdp", split_axis=2, concat_axis=0, tiled=True),
    )
    sum_down = combine_tiles(group_lang, language_owner, part_down)
    sum_up = combine_tiles(group_lang, language_owner, partial_up)
    sum_down, sum_up = lax.psum((sum_down, sum_up), "dp")
    grad_down = (sum_down * adapter_factor).astype(jnp.bfloat16)
    grad_up = (sum_up * adapter_factor).astype(jnp.bfloat16)
    return (input_gradient, grad_down, grad_up)


def solution(mesh):
    return jax.shard_map(
        on_device,
        mesh=mesh,
        in_specs=(
            P(("fsdp", "dp", "owner"), None),
            P(("fsdp", "dp", "owner"), None),
            P(),
            P(),
            P("fsdp", None),
            P("owner", None, "fsdp"),
            P("owner", None, "fsdp"),
        ),
        out_specs=(
            P(("fsdp", "dp", "owner"), None),
            P("owner", None, "fsdp"),
            P("owner", None, "fsdp"),
        ),
        check_vma=False,
    )
```

profile of v0, /device:TPU:1, one launch (start us, length us, event | category | flops | bytes accessed | tf_op | source)
XLA Modules:
  0.0 609.0 jit_solution(11307650791264360045)
XLA Ops:
  7.2 0.0 copy-start
  7.2 0.0 copy-start.1
  7.2 0.0 copy-start.2
  7.2 0.0 all-gather.6.cloned.1.call-start
  7.2 0.7 all-gather.6.cloned.1.call-update
  7.9 0.0 all-gather.8.cloned.1.call-start
  8.0 0.7 all-gather.8.cloned.1.call-update
  8.7 0.0 copy-done.1
  8.7 0.6 gather_fusion.4
  9.4 0.0 copy-done.2
  9.4 0.6 gather_fusion.3
  10.1 0.1 iota_compare_fusion.1
  10.1 51.1 %all-gather.6.cloned.1.call-done = bf16[32,32,2048]{2,1,0:T(8,128)(2,1)} async-done(((bf16[32,32,512]{2,1,0:T(8,128)(2,1)}), bf16[32,32,2048]{2,1,0:T(8,128)(2,1)}) %all-gather.6.cloned.1.call-update) | async-done | bytes 4194320 | tf_op jit(solution)/shard_map/all_gather | solution.py:51
  61.2 2.8 gather_fusion
  64.0 0.0 copy-done
  64.0 0.8 fusion
  64.8 4.5 fusion.23
  69.3 8.0 %copy.18 = f32[4,32,4608]{1,0,2:T(4,128)} copy(f32[4,32,4608]{2,1,0:T(8,128)} %fusion.23) | data formatting | bytes 4718592 | tf_op jit(solution)/shard_map/ktr,ktd->krd/dot_general | solution.py:84
  77.3 9.4 %reshape.173 = f32[4,1,147456]{2,1,0:T(1,128)} reshape(f32[4608,4,32]{2,1,0:T(4,128)} %bitcast.34) | data formatting | bytes 4718592
  86.7 4.5 all-to-all-start
  91.3 0.1 iota_add_fusion
  91.3 0.1 add.117
  91.4 89.1 %all-gather.8.cloned.1.call-done = bf16[32,32,4608]{2,1,0:T(8,128)(2,1)} async-done(((bf16[32,32,1152]{2,1,0:T(8,128)(2,1)}), bf16[32,32,4608]{2,1,0:T(8,128)(2,1)}) %all-gather.8.cloned.1.call-update) | async-done | bytes 9437200 | tf_op jit(solution)/shard_map/all_gather | solution.py:50
  180.5 4.3 gather_fusion.1
  184.8 5.3 fusion.2
  190.1 4.5 copy.20
  194.6 5.3 reshape.175
  200.0 0.0 all-to-all-done
  200.0 4.3 all-to-all-start.1
  204.2 0.2 all-reduce.3.cloned.1.call-start
  204.5 0.1 add.115
  204.5 0.7 gather_fusion.2
  205.2 0.6 broadcast.209
  205.8 9.4 %reduce = f32[4,147456]{1,0:T(4,128)} reduce(f32[4,1,147456]{2,1,0:T(1,128)} %all-to-all-done, f32[]{:T(128)} %broadcast.209), dimensions={1}, to_apply=%all_to_all.26.reduce_sub_computation | reduce | bytes 4718596 | tf_op jit(solution)/shard_map/all_to_all | solution.py:91
  215.2 10.4 %reshape.174 = f32[4608,4,32]{2,1,0:T(4,128)} reshape(f32[4,147456]{1,0:T(4,128)} %reduce) | data formatting | bytes 4718592
  225.7 9.1 %copy.19 = f32[4,32,4,1152]{3,0,2,1:T(4,128)} copy(f32[4,32,4,1152]{1,0,3,2:T(4,128)} %bitcast.35) | data formatting | bytes 4718592 | tf_op jit(solution)/shard_map/all_to_all | solution.py:91
  234.8 3.6 all_to_all.29
  238.4 6.0 fusion.11
  244.4 0.0 all-to-all-done.1
  244.4 5.5 reduce.1
  249.9 5.5 reshape.176
  255.4 4.6 copy.21
  259.9 2.6 all_to_all.33
  262.5 3.6 fusion.9
  266.1 0.0 all-reduce.3.cloned.1.call-update
  266.2 0.0 all-gather.4.cloned.1.call-start
  266.2 0.5 all-gather.4.cloned.1.call-update
  266.8 138.0 %all-reduce.3.cloned.1.call-done = (f32[32,32,1152]{2,0,1:T(8,128)}, f32[32,32,512]{2,0,1:T(8,128)}) async-done(((f32[32,32,1152]{2,0,1:T(8,128)}, f32[32,32,512]{2,0,1:T(8,128)}), (f32[32,32,1152]{2,0,1:T(8,128)}, f32[32,32,512]{2,0,1:T(8,128)})) %all-reduce.3.cloned.1.call-update) | async-done | bytes 6815760 | tf_op jit(solution)/shard_map/psum | solution.py:96
  404.7 2.7 multiply_convert_fusion
  407.5 0.0 copy-start.3
  407.5 2.1 copy.22
  409.6 0.0 copy-done.3
  409.6 0.3 multiply_convert_fusion.1
  409.9 1.5 copy.23
  411.5 168.9 %all-gather.4.cloned.1.call-done = bf16[4608,2048]{1,0:T(8,128)(2,1)} async-done(((bf16[1152,2048]{1,0:T(8,128)(2,1)}), bf16[4608,2048]{1,0:T(8,128)(2,1)}) %all-gather.4.cloned.1.call-update) | async-done | bytes 18874384 | tf_op jit(solution)/shard_map/all_gather | solution.py:69
  580.4 16.1 %fusion.22 = f32[512,4608]{1,0:T(8,128)} fusion(bf16[512,2048]{1,0:T(8,128)(2,1)S(1)} %copy-done, bf16[4608,2048]{1,0:T(8,128)(2,1)} %all-gather.4.cloned.1.call-done), kind=kOutput, calls=%fused_computation.46 | convolution fusion | flops 9663676416 | bytes 30408704 | tf_op jit(solution)/shard_map/dot_general | solution.py:67
  596.4 6.0 select_convert_fusion
  (9 shorter events, 0.1 us)
Async XLA Ops:
  7.2 56.8 %copy-start = (bf16[512,2048]{1,0:T(8,128)(2,1)S(1)}, bf16[512,2048]{1,0:T(8,128)(2,1)}, u32[]{:S(2)}) copy-start(bf16[512,2048]{1,0:T(8,128)(2,1)} %param.10) | copy-start | bytes 6291460
  7.2 1.5 copy-start.1
  7.2 2.2 copy-start.2
  7.2 54.0 %all-gather.6.cloned.1.call-start = ((), (), s32[]{:S(2)}) async-start(), calls=%async_computation.3 | async-start | bytes 5242880 | tf_op jit(solution)/shard_map/all_gather | solution.py:51
  7.9 172.6 %all-gather.8.cloned.1.call-start = ((), (), s32[]{:S(2)}) async-start(), calls=%async_computation.4 | async-start | bytes 11796480 | tf_op jit(solution)/shard_map/all_gather | solution.py:50
  86.7 113.2 %all-to-all-start = ((f32[4,1,147456]{2,1,0:T(1,128)}), f32[4,1,147456]{2,1,0:T(1,128)}, u32[]{:S(2)}, u32[]{:S(2)}) async-start(f32[4,1,147456]{2,1,0:T(1,128)} %reshape.173), calls=%async_computation | async-start | bytes 4718592 | tf_op jit(solution)/shard_map/all_to_all | solution.py:91
  200.0 44.4 %all-to-all-start.1 = ((f32[4,1,65536]{2,1,0:T(1,128)}), f32[4,1,65536]{2,1,0:T(1,128)}, u32[]{:S(2)}, u32[]{:S(2)}) async-start(f32[4,1,65536]{2,1,0:T(1,128)} %reshape.175), calls=%async_computation.1 | async-start | bytes 2097152 | tf_op jit(solution)/shard_map/all_to_all | solution.py:92
  204.2 200.5 %all-reduce.3.cloned.1.call-start = ((), (), s32[]{:S(2)}) async-start(), calls=%async_computation.5 | async-start | bytes 13631488 | tf_op jit(solution)/shard_map/psum | solution.py:96
  266.2 314.2 %all-gather.4.cloned.1.call-start = ((), (), s32[]{:S(2)}) async-start(), calls=%async_computation.2 | async-start | bytes 23592960 | tf_op jit(solution)/shard_map/all_gather | solution.py:69
  407.5 2.1 copy-start.3
Sparse Core Ops, SparseCore 0:
  9.7 51.4 all-gather.5
  62.9 117.5 all-gather.7
  266.3 138.4 all-reduce.2
  406.3 174.0 all-gather.3
where the time goes:
time: 610 us; the launch traced here: 609 us
  waiting for transfers between devices  449 us (74%)
  local copies, waits for them, and re-layouts  76.5 us (13%)
  matrix products  42.3 us (7%)
  other arithmetic  18.2 us (3%)
  between operations  13.9 us (2%)
  starting transfers between devices  9.11 us (1%)
    all_gather x1, waiting for transfers between devices, on_device(): lax.all_gather(frozen_weight, 'fsdp', axis=0, tiled=True)  169 us
    psum x1, waiting for transfers between devices, on_device(): sum_down, sum_up = lax.psum((sum_down, sum_up), 'dp')  138 us
    all_gather x1, waiting for transfers between devices, on_device(): lax.all_gather(adapter_down, 'fsdp', axis=2, tiled=True)  89.1 us
    all_gather x1, waiting for transfers between devices, on_device(): lax.all_gather(adapter_up, 'fsdp', axis=2, tiled=True)  51.1 us
    unnamed x14, local copies, waits for them, and re-layouts  34.3 us
    dot_general x1, matrix products, on_device(): jnp.dot(output_gradient, lax.all_gather(frozen_weight, 'fsdp', axis=0, ti...  16.1 us
    all_to_all x3, local copies, waits for them, and re-layouts, on_device(): lax.all_to_all(part_down, 'fsdp', split_axis=2, concat_axis=0, tiled=True)  13.3 us
  transfers between devices with their start and end apart: 6, of which 4 were waited for; matrix products, arithmetic and copies ran while one was open for 15% of the time, Pallas kernels for 0%

commit v1 on v0

v1 whole, which is shorter than its diff:
```python
import functools

import jax
import jax.numpy as jnp
from jax import lax
from jax.experimental import pallas as pl
from jax.experimental.pallas import tpu as pltpu
from jax.sharding import PartitionSpec as P

MESH = pl.DeviceIdType.MESH
NT = (((1,), (1,)), ((), ()))
NN = (((1,), (0,)), ((), ()))

TILE = 128
TILES = 4
RANK = 32
ROWS = TILES * RANK
LANGS = 32
YN = 4
CHIPS = 8
DP = 16
T = TILE * TILES
D_ALL, Q_ALL = 4608, 2048
D_SH, Q_SH = D_ALL // YN, Q_ALL // YN
SUB = 32
BLK = 4 * SUB
HALF = 4 * BLK
TAIL = D_SH - 2 * HALF


def dot(a, b, dims=NN):
    return lax.dot_general(a, b, dims, preferred_element_type=jnp.float32)


def permutation(shape):
    i = lax.broadcasted_iota(jnp.int32, shape, 0)
    j = lax.broadcasted_iota(jnp.int32, shape, 1)
    k, q, r = lax.div(lax.rem(j, 16), 4), lax.div(j, 16), lax.rem(j, 4)
    return (i == k * RANK + q * 4 + r).astype(jnp.float32).astype(jnp.bfloat16)


def main_kernel(
    lang, live, lang_cols, tokens, grad, weight, adown, aup,
    ig, gd, gu,
    wbuf, wtail, wl, tok, og, adv, auv, su, sd, uu, dd, spd, spu, r1d, r1u, r2d, r2u, gdv, guv, igv, b2, btp, htp,
    in_sem, y_s, y_r, a_s, a_r, b_s, b_r, f_s, f_r, c_s, c_r, t_s, t_r, tc_s, tc_r,
    u_s, u_r, d_s, d_r, pd_s, pd_r, pu_s, pu_r, xd_s, xd_r, xu_s, xu_r, ag_s, ag_r, agc_s, agc_r, own_s, out_s,
):
    f, e, o = lax.axis_index("fsdp"), lax.axis_index("dp"), lax.axis_index("owner")
    q, c = lax.div(e, 2), lax.rem(e, 2)
    x, z = lax.rem(q, 4), o * 2 + lax.div(q, 4)
    pa = x * (1 - c) + z * c
    pb = z * (1 - c) + x * c

    def mod(v, n):
        return lax.rem(v + n, n)

    def at_ab(da, db):
        a, b = mod(pa + da, 4), mod(pb + db, 4)
        xx, zz = a * (1 - c) + b * c, b * (1 - c) + a * c
        return (f, lax.rem(zz, 2) * 8 + xx * 2 + c, lax.div(zz, 2))

    def at_y(s):
        return (mod(f + s, 4), e, o)

    def at_dp(chip, core):
        return (f, chip * 2 + core, o)

    other = at_dp(q, 1 - c)

    def rcopy(src, dst, ssem, rsem, dev):
        return pltpu.make_async_remote_copy(
            src_ref=src, dst_ref=dst, send_sem=ssem, recv_sem=rsem, device_id=dev, device_id_type=MESH
        )

    def await_ref(ref, sem):
        pltpu.make_async_copy(ref, ref, sem).wait()

    sends = []

    def send(*args):
        cp = rcopy(*args)
        cp.start()
        sends.append(cp)

    loads = [
        pltpu.make_async_copy(s, d, in_sem.at[i])
        for i, (s, d) in enumerate(((aup, auv), (adown, adv), (grad, og), (tokens, tok), (weight, wl)))
    ]
    for cp in loads:
        cp.start()

    barrier = pltpu.get_barrier_semaphore()
    peers = [at_y(s) for s in (1, 2, 3)]
    peers += [at_ab(s, 0) for s in (1, 2, 3)] + [at_ab(0, 1), at_ab(0, -1)]
    peers += [(f, mod(e + s, DP), o) for s in range(1, DP)]
    for dev in peers:
        pl.semaphore_signal(barrier, inc=1, device_id=dev, device_id_type=MESH)
    pl.semaphore_wait(barrier, len(peers))

    sub0 = pl.multiple_of(pa * SUB, SUB)
    piece = pl.multiple_of(c * HALF + pb * BLK + pa * SUB, SUB)
    for s in (2, 1, 3):
        send(
            weight.at[pl.ds(piece, SUB)], wbuf.at[3 - s, 0, c, pl.ds(sub0, SUB)],
            y_s.at[s - 1], y_r.at[3 - s], at_y(s),
        )

    def choose(table, s, out):
        first = ((mod(f + s, 4) * DP + e) * 2 + o) * TILES
        for k in range(TILES):
            out[pl.ds(k * RANK, RANK), :] = table[lax.rem(lang[first + k], LANGS)]

    loads[0].wait()
    for s in (2, 1, 3):
        choose(auv, s, su.at[s - 1])
        send(su.at[s - 1], uu.at[f], u_s.at[s - 1], u_r.at[s - 1], at_y(s))
    choose(auv, 0, uu.at[f])
    loads[1].wait()
    for s in (2, 1, 3):
        choose(adv, s, sd.at[s - 1])
        send(sd.at[s - 1], dd.at[f], d_s.at[s - 1], d_r.at[s - 1], at_y(s))
    choose(adv, 0, dd.at[f])

    loads[2].wait()
    own = ((f * DP + e) * 2 + o) * TILES
    slot = lax.broadcasted_iota(jnp.int32, (TILE, Q_ALL), 0)
    for k in range(TILES):
        rows = pl.ds(k * TILE, TILE)
        og[rows, :] = jnp.where(slot < live[own + k], og[rows, :].astype(jnp.float32), 0.0).astype(jnp.bfloat16)

    def b_sends(s):
        rows = pl.ds(pl.multiple_of(mod(pa - s, 4) * SUB, SUB), SUB)
        unit = wbuf.at[:, 0, c, rows]
        send(unit, wbuf.at[:, 3, c, rows], b_s.at[0, s], b_r.at[0, s], at_ab(0, 1))
        send(unit, wbuf.at[:, 1, c, rows], b_s.at[1, s], b_r.at[1, s], at_ab(0, -1))

    for i in range(3):
        await_ref(wbuf.at[i, 0, c, pl.ds(sub0, SUB)], y_r.at[i])
    own_unit = wbuf.at[:, 0, c, pl.ds(sub0, SUB)]
    for s in (2, 1, 3):
        send(own_unit, own_unit, a_s.at[s - 1], a_r.at[s - 1], at_ab(s, 0))
    b_sends(0)

    for s in (1, 3, 2):
        await_ref(uu.at[mod(f - s, 4)], u_r.at[s - 1])
    j = lax.broadcasted_iota(jnp.int32, (ROWS, T), 0)
    t = lax.broadcasted_iota(jnp.int32, (ROWS, T), 1)
    limit = jnp.where(
        t < 2 * TILE,
        jnp.where(t < TILE, live[own], live[own + 1]),
        jnp.where(t < 3 * TILE, live[own + 2], live[own + 3]),
    )
    mask = (lax.div(j, RANK) == lax.div(t, TILE)) & (lax.rem(t, TILE) < limit)
    perm_t = permutation((ROWS, ROWS)).astype(jnp.float32).T.astype(jnp.bfloat16)

    def rows_by_chip(v):
        v = jnp.where(mask, v, 0.0).astype(jnp.bfloat16)
        return dot(perm_t, v).astype(jnp.bfloat16)

    bt = jnp.zeros((ROWS, T), jnp.float32)
    bb = jnp.zeros((T, ROWS), jnp.float32)
    for y in range(YN):
        bt += dot(uu[y], og[:, y * Q_SH : (y + 1) * Q_SH], NT)
        bb += dot(og[:, y * Q_SH : (y + 1) * Q_SH], uu[y], NT)
    tt = lax.broadcasted_iota(jnp.int32, (T, ROWS), 0)
    jj = lax.broadcasted_iota(jnp.int32, (T, ROWS), 1)
    bb = jnp.where(lax.div(jj, RANK) == lax.div(tt, TILE), bb, 0.0).astype(jnp.bfloat16)
    b2[...] = (bb.astype(jnp.float32) * 2.0).astype(jnp.bfloat16)
    btp[...] = rows_by_chip(bt)

    loads[3].wait()
    for s in (2, 1, 3, 0):
        y = mod(f + s, 4)
        part = dot(btp[...], tok[:, pl.ds(pl.multiple_of(y * D_SH, TILE), D_SH)]).astype(jnp.bfloat16)
        if s:
            spd[s - 1] = part
            send(spd.at[s - 1], r1d.at[f], pd_s.at[s - 1], pd_r.at[s - 1], at_y(s))
        else:
            r1d[f] = part

    def spread(core, r1, r2, s, ssem, rsem):
        y = mod(f - s, 4)

        def one(i, _):
            chip = lax.rem(q + i, CHIPS)
            src = r1.at[y, pl.ds(pl.multiple_of(chip * 16, 16), 16)]

            @pl.when((i > 0) | (c != core))
            def _():
                rcopy(src, r2.at[e, y], ssem.at[s, i], rsem, at_dp(chip, core)).start()

            @pl.when((i == 0) & (c == core))
            def _():
                pltpu.make_async_copy(src, r2.at[e, y], rsem).start()

            return 0

        lax.fori_loop(0, CHIPS, one, 0)

    def spread_done(core, r1, r2, ssem):
        def one(i, _):
            s, t = lax.div(i, CHIPS), lax.rem(i, CHIPS)

            @pl.when((t > 0) | (c != core))
            def _():
                src = r1.at[0, pl.ds(0, 16)]
                rcopy(src, r2.at[0, 0], ssem.at[s, t], ssem.at[s, t], at_dp(q, 1 - c)).wait_send()

            return 0

        lax.fori_loop(0, YN * CHIPS, one, 0)

    spread(0, r1d, r2d, 0, xd_s, xd_r.at[0])

    def columns(w, y, first, width):
        d = dd[y, :, pl.ds(first, width)]
        return (dot(og[...], w, NT) + dot(b2[...], d)).astype(jnp.bfloat16)

    def put(y, first, width, value):
        igv[:, pl.ds(pl.multiple_of(y * D_SH + first, TILE), width)] = value

    loads[4].wait()

    def local_chunk(i, _):
        first = pl.multiple_of(i * 384, TILE)
        put(f, first, 384, columns(wl[pl.ds(first, 384), :], f, first, 384))
        return 0

    lax.fori_loop(0, D_SH // 384, local_chunk, 0)

    for s in (1, 3, 2):
        rows = pl.ds(pl.multiple_of(mod(pa - s, 4) * SUB, SUB), SUB)
        await_ref(wbuf.at[:, 0, c, rows], a_r.at[s - 1])
        b_sends(s)

    def to_other(rel):
        send(wbuf.at[:, rel, c], wbuf.at[:, rel, c], c_s.at[rel], c_r.at[rel], other)

    to_other(0)

    def pass_on(s):
        rows = pl.ds(pl.multiple_of(mod(pa - s, 4) * SUB, SUB), SUB)
        await_ref(wbuf.at[:, 3, c, rows], b_r.at[0, s])
        await_ref(wbuf.at[:, 1, c, rows], b_r.at[1, s])
        if s in (0, 2):
            send(wbuf.at[:, 3, c, rows], wbuf.at[:, 2, c, rows], f_s.at[s], f_r.at[s], at_ab(0, 1))
        else:
            send(wbuf.at[:, 1, c, rows], wbuf.at[:, 2, c, rows], f_s.at[s], f_r.at[s], at_ab(0, -1))

    pass_on(0)

    for s in (1, 3, 2):
        await_ref(dd.at[mod(f - s, 4)], d_r.at[s - 1])
    ht = jnp.zeros((ROWS, T), jnp.float32)
    for y in range(YN):
        ht += dot(dd[y], tok[:, y * D_SH : (y + 1) * D_SH], NT)
    htp[...] = rows_by_chip(ht)
    for s in (2, 1, 3, 0):
        y = mod(f + s, 4)
        part = dot(htp[...], og[:, pl.ds(pl.multiple_of(y * Q_SH, TILE), Q_SH)]).astype(jnp.bfloat16)
        if s:
            spu[s - 1] = part
            send(spu.at[s - 1], r1u.at[f], pu_s.at[s - 1], pu_r.at[s - 1], at_y(s))
        else:
            r1u[f] = part
    spread(1, r1u, r2u, 0, xu_s, xu_r.at[0])

    mine = pl.ds(pl.multiple_of(c * (TAIL // 2), TAIL // 2), TAIL // 2)
    tail_rows = pl.ds(pl.multiple_of(2 * HALF + c * (TAIL // 2), TAIL // 2), TAIL // 2)
    for s in (2, 1, 3):
        send(weight.at[tail_rows], wtail.at[3 - s, mine], t_s.at[s - 1], t_r.at[3 - s], at_y(s))

    for s in (1, 3, 2):
        pass_on(s)
    for rel in (1, 3):
        to_other(rel)

    for s in (1, 3, 2):
        await_ref(r1d.at[mod(f - s, 4)], pd_r.at[s - 1])
        spread(0, r1d, r2d, s, xd_s, xd_r.at[0])

    def block(rel):
        await_ref(wbuf.at[:, rel, 1 - c], c_r.at[rel])

        def one(i, _):
            y = mod(f + i + 1, 4)
            w = wbuf[i, rel].reshape(2 * BLK, Q_ALL)
            first0 = pl.multiple_of(mod(z + rel, 4) * BLK, BLK)
            first1 = pl.multiple_of(HALF + mod(x + rel, 4) * BLK, BLK)
            acc = dot(og[...], w, NT)
            add0 = dot(b2[...], dd[y, :, pl.ds(first0, BLK)])
            add1 = dot(b2[...], dd[y, :, pl.ds(first1, BLK)])
            put(y, first0, BLK, (acc[:, :BLK] + add0).astype(jnp.bfloat16))
            put(y, first1, BLK, (acc[:, BLK:] + add1).astype(jnp.bfloat16))
            return 0

        lax.fori_loop(0, 3, one, 0)

    block(0)

    for s in (1, 3, 2):
        await_ref(r1u.at[mod(f - s, 4)], pu_r.at[s - 1])
        spread(1, r1u, r2u, s, xu_s, xu_r.at[0])

    block(1)
    block(3)

    def add_up(r2, rsem, gv, g):
        await_ref(r2, rsem)
        m = lax.broadcasted_iota(jnp.int32, (CHIPS * 16, DP * YN * 16), 0)
        n = lax.broadcasted_iota(jnp.int32, (CHIPS * 16, DP * YN * 16), 1)
        hit = (lang_cols[o] - o * LANGS == lax.div(m, 4)) & (lax.rem(n, 4) == lax.rem(m, 4))
        pick = hit.astype(jnp.float32).astype(jnp.bfloat16)
        width = r2.shape[-1]
        total = dot(pick, r2[...].reshape(DP * YN * 16, width))
        gv[...] = (total * (2.0 / 256.0)).astype(jnp.bfloat16)
        for s in range(1, CHIPS):
            rcopy(gv, g.at[q], ag_s.at[s - 1], ag_r.at[s - 1], at_dp(mod(q + s, CHIPS), c)).start()
        rcopy(gv, g.at[q], agc_s.at[0], agc_r.at[0], other).start()
        pltpu.make_async_copy(gv, g.at[q], own_s.at[0]).start()

    def gather_up(gv, g):
        for s in range(1, CHIPS):
            part = g.at[mod(q - s, CHIPS)]
            await_ref(part, ag_r.at[s - 1])
            rcopy(part, part, agc_s.at[s], agc_r.at[s], other).start()
        await_ref(gv, own_s.at[0])
        for s in range(1, CHIPS):
            rcopy(gv, g.at[q], ag_s.at[s - 1], ag_r.at[s - 1], other).wait_send()
        for s in range(CHIPS):
            rcopy(gv, g.at[q], agc_s.at[s], agc_r.at[s], other).wait_send()

    def from_other(g):
        for s in range(CHIPS):
            await_ref(g.at[mod(q - s, CHIPS)], agc_r.at[s])

    @pl.when(c == 0)
    def _():
        add_up(r2d, xd_r.at[0], gdv, gd)

    for s in range(4):
        rows = pl.ds(pl.multiple_of(mod(pa - s, 4) * SUB, SUB), SUB)
        await_ref(wbuf.at[:, 2, c, rows], f_r.at[s])
    to_other(2)
    for i in range(3):
        await_ref(wtail.at[i, mine], t_r.at[i])
    send(wtail.at[:, mine], wtail.at[:, mine], tc_s.at[0], tc_r.at[0], other)

    @pl.when(c == 1)
    def _():
        add_up(r2u, xu_r.at[0], guv, gu)

    block(2)
    theirs = pl.ds(pl.multiple_of((1 - c) * (TAIL // 2), TAIL // 2), TAIL // 2)
    await_ref(wtail.at[:, theirs], tc_r.at[0])

    def tail_chunk(i, _):
        y = mod(f + i + 1, 4)
        put(y, 2 * HALF, TAIL, columns(wtail[i], y, 2 * HALF, TAIL))
        return 0

    lax.fori_loop(0, 3, tail_chunk, 0)
    out = pltpu.make_async_copy(igv, ig, out_s.at[0])
    out.start()

    @pl.when(c == 0)
    def _():
        gather_up(gdv, gd)
        from_other(gu)

    @pl.when(c == 1)
    def _():
        gather_up(guv, gu)
        from_other(gd)

    for cp in sends:
        cp.wait_send()
    spread_done(0, r1d, r2d, xd_s)
    spread_done(1, r1u, r2u, xu_s)
    out.wait()


def finish_kernel(gd, gu, ig_in, down, up, ig, sem):
    cp = pltpu.make_async_copy(ig_in, ig, sem)
    cp.start()
    perm = permutation((ROWS, ROWS))
    for src, dst in ((gd, down), (gu, up)):
        width = src.shape[-1]
        for g in range(CHIPS):
            rows = src[:, g * 16 : (g + 1) * 16, :].reshape(ROWS, width)
            dst[g * 4 : (g + 1) * 4] = dot(perm, rows).astype(jnp.bfloat16).reshape(4, RANK, width)
    cp.wait()


def on_device(tokens, output_gradient, tile_language, tile_live_count, frozen_weight, adapter_down, adapter_up):
    bf = jnp.bfloat16
    by_owner = tile_language.reshape(YN, DP, 2, TILES).transpose(2, 1, 0, 3)
    lang_cols = jnp.repeat(by_owner.reshape(2, 1, DP * YN * TILES), 4, axis=2)
    hbm, smem, vmem = (pl.BlockSpec(memory_space=s) for s in (pl.ANY, pltpu.SMEM, pltpu.VMEM))
    sem = pltpu.SemaphoreType.DMA

    def sems(*shapes):
        return [sem(s) for s in shapes]

    ig, gd, gu = pl.pallas_call(
        main_kernel,
        out_shape=(
            jax.ShapeDtypeStruct((T, D_ALL), bf),
            jax.ShapeDtypeStruct((CHIPS, CHIPS * 16, D_SH), bf),
            jax.ShapeDtypeStruct((CHIPS, CHIPS * 16, Q_SH), bf),
        ),
        in_specs=[smem, smem, vmem, hbm, hbm, hbm, hbm, hbm],
        out_specs=(hbm, hbm, hbm),
        scratch_shapes=[
            pltpu.VMEM((3, 4, 2, BLK, Q_ALL), bf),
            pltpu.VMEM((3, TAIL, Q_ALL), bf),
            pltpu.VMEM((D_SH, Q_ALL), bf),
            pltpu.VMEM((T, D_ALL), bf),
            pltpu.VMEM((T, Q_ALL), bf),
            pltpu.VMEM((LANGS, RANK, D_SH), bf),
            pltpu.VMEM((LANGS, RANK, Q_SH), bf),
            pltpu.VMEM((3, ROWS, Q_SH), bf),
            pltpu.VMEM((3, ROWS, D_SH), bf),
            pltpu.VMEM((YN, ROWS, Q_SH), bf),
            pltpu.VMEM((YN, ROWS, D_SH), bf),
            pltpu.VMEM((3, ROWS, D_SH), bf),
            pltpu.VMEM((3, ROWS, Q_SH), bf),
            pltpu.VMEM((YN, ROWS, D_SH), bf),
            pltpu.VMEM((YN, ROWS, Q_SH), bf),
            pltpu.VMEM((DP, YN, 16, D_SH), bf),
            pltpu.VMEM((DP, YN, 16, Q_SH), bf),
            pltpu.VMEM((CHIPS * 16, D_SH), bf),
            pltpu.VMEM((CHIPS * 16, Q_SH), bf),
            pltpu.VMEM((T, D_ALL), bf),
            pltpu.VMEM((T, ROWS), bf),
            pltpu.VMEM((ROWS, T), bf),
            pltpu.VMEM((ROWS, T), bf),
            *sems((5,), (3,), (3,), (3,), (3,), (2, 4), (2, 4), (4,), (4,), (4,), (4,), (3,), (3,), (1,), (1,)),
            *sems((3,), (3,), (3,), (3,), (3,), (3,), (3,), (3,), (4, 8), (1,), (4, 8), (1,)),
            *sems((7,), (7,), (8,), (8,), (1,), (1,)),
        ],
        compiler_params=pltpu.CompilerParams(
            collective_id=0, has_side_effects=True, vmem_limit_bytes=58 * 2**20
        ),
        cost_estimate=pl.CostEstimate(flops=12 * 10**9, bytes_accessed=40 * 10**6, transcendentals=0),
        name="exchange",
    )(tile_language, tile_live_count, lang_cols, tokens, output_gradient, frozen_weight, adapter_down, adapter_up)
    down, up, ig = pl.pallas_call(
        finish_kernel,
        out_shape=(
            jax.ShapeDtypeStruct((LANGS, RANK, D_SH), bf),
            jax.ShapeDtypeStruct((LANGS, RANK, Q_SH), bf),
            jax.ShapeDtypeStruct((T, D_ALL), bf),
        ),
        in_specs=[vmem, vmem, hbm],
        out_specs=(vmem, vmem, hbm),
        scratch_shapes=[sem],
        compiler_params=pltpu.CompilerParams(vmem_limit_bytes=40 * 2**20),
        name="finish",
    )(gd, gu, ig)
    return ig, down, up


def solution(mesh):
    tok = P(("fsdp", "dp", "owner"), None)
    adapter = P("owner", None, "fsdp")
    return jax.shard_map(
        on_device,
        mesh=mesh,
        in_specs=(tok, tok, P(), P(), P("fsdp", None), adapter, adapter),
        out_specs=(tok, adapter, adapter),
        check_vma=False,
    )
```

time: 610 us -> 115 us (0.19)
  the two profiles are of different devices: /device:TPU:1 before, /device:TPU:57 now
where the time goes in v1:
time: 115 us
  Pallas kernels  107 us (93%)
  local copies, waits for them, and re-layouts  7.12 us (6%)
    pallas_call x1, Pallas kernels, on_device(): pl.pallas_call(main_kernel, out_shape=(jax.ShapeDtypeStruct((T, D_ALL), b...  103 us
    unnamed x6, local copies, waits for them, and re-layouts  5.22 us
    pallas_call x1, Pallas kernels, on_device(): pl.pallas_call(finish_kernel, out_shape=(jax.ShapeDtypeStruct((LANGS, RAN...  4.17 us

profile of v1, /device:TPU:57, one launch (start us, length us, event | category | flops | bytes accessed | tf_op | source)
XLA Modules:
  0.0 114.5 jit_solution(1275522203690863457)
XLA Ops:
  0.6 0.8 reshape.18
  1.5 0.1 reshape.19
  1.6 0.1 broadcast_in_dim.5
  1.8 0.8 broadcast_in_dim.7.lang_cols
  2.6 102.6 %exchange.1 = (bf16[512,4608]{1,0:T(8,128)(2,1)}, bf16[8,128,1152]{2,1,0:T(8,128)(2,1)}, bf16[8,128,512]{2,1,0:T(8,128)(2,1)}) custom-call(s32[512]{0:T(512)} %lang.1, s32[512]{0:T(512)} %live.1, s32[2,1,1024]{2,1,0:T(1,128)} %broadcast_in_dim.7.lang_cols, bf16[512,4608]{1,0:T(8,128)(2,1)} %tokens.1, bf16[512,2048]{1,0:T(8,128)(2,1)} %grad.1, ...), custom_call_target="tpu_custom_call" | custom-call | flops 12000000000 | bytes 40000000 | tf_op jit(solution)/shard_map/exchange/pallas_call | solution.py:406
  105.1 0.0 copy-start
  105.1 2.3 %copy-done = bf16[512,4608]{1,0:T(8,128)(2,1)S(1)} copy-done((bf16[512,4608]{1,0:T(8,128)(2,1)S(1)}, bf16[512,4608]{1,0:T(8,128)(2,1)}, u32[]{:S(2)}) %copy-start) | copy-done | bytes 4718616
  107.5 0.0 copy-start.1
  107.5 1.7 %copy-done.1 = bf16[8,128,1152]{2,1,0:T(8,128)(2,1)S(1)} copy-done((bf16[8,128,1152]{2,1,0:T(8,128)(2,1)S(1)}, bf16[8,128,1152]{2,1,0:T(8,128)(2,1)}, u32[]{:S(2)}) %copy-start.1) | copy-done | bytes 2359320
  109.1 0.0 copy-start.2
  109.1 1.2 %copy-done.2 = bf16[8,128,512]{2,1,0:T(8,128)(2,1)S(1)} copy-done((bf16[8,128,512]{2,1,0:T(8,128)(2,1)S(1)}, bf16[8,128,512]{2,1,0:T(8,128)(2,1)}, u32[]{:S(2)}) %copy-start.2) | copy-done | bytes 1048600
  110.3 4.2 %finish.1 = (bf16[32,32,1152]{2,1,0:T(8,128)(2,1)}, bf16[32,32,512]{2,1,0:T(8,128)(2,1)}, bf16[512,4608]{1,0:T(8,128)(2,1)}) custom-call(bf16[8,128,1152]{2,1,0:T(8,128)(2,1)S(1)} %copy-done.1, bf16[8,128,512]{2,1,0:T(8,128)(2,1)S(1)} %copy-done.2, bf16[512,4608]{1,0:T(8,128)(2,1)S(1)} %copy-done), custom_call_target="tpu_custom_call" | custom-call | tf_op jit(solution)/shard_map/finish/pallas_call | solution.py:449
  (1 shorter events, 0.0 us)
Async XLA Ops:
  105.1 2.3 %copy-start = (bf16[512,4608]{1,0:T(8,128)(2,1)S(1)}, bf16[512,4608]{1,0:T(8,128)(2,1)}, u32[]{:S(2)}) copy-start(bf16[512,4608]{1,0:T(8,128)(2,1)} %get-tuple-element.11.ig_in) | copy-start | bytes 14155780
  107.5 1.7 %copy-start.1 = (bf16[8,128,1152]{2,1,0:T(8,128)(2,1)S(1)}, bf16[8,128,1152]{2,1,0:T(8,128)(2,1)}, u32[]{:S(2)}) copy-start(bf16[8,128,1152]{2,1,0:T(8,128)(2,1)} %get-tuple-element.9.gd) | copy-start | bytes 7077892
  109.1 1.2 %copy-start.2 = (bf16[8,128,512]{2,1,0:T(8,128)(2,1)S(1)}, bf16[8,128,512]{2,1,0:T(8,128)(2,1)}, u32[]{:S(2)}) copy-start(bf16[8,128,512]{2,1,0:T(8,128)(2,1)} %get-tuple-element.10.gu) | copy-start | bytes 3145732

commit v2 on v1

v2 whole, which is shorter than its diff:
```python
import functools

import jax
import jax.numpy as jnp
from jax import lax
from jax.experimental import pallas as pl
from jax.experimental.pallas import tpu as pltpu
from jax.sharding import PartitionSpec as P

MESH = pl.DeviceIdType.MESH
NT = (((1,), (1,)), ((), ()))
NN = (((1,), (0,)), ((), ()))

TILE = 128
TILES = 4
RANK = 32
ROWS = TILES * RANK
LANGS = 32
YN = 4
CHIPS = 8
T = TILE * TILES
D_ALL, Q_ALL = 4608, 2048
D_SH, Q_SH = D_ALL // YN, Q_ALL // YN
G_ALL = D_SH + Q_SH
CUT = 896
SUB = 112
HALF = 4 * SUB
TAIL = D_SH - 2 * HALF
MINE = TAIL // 2
LOCAL = 384
SLOTS = (1, 3, 2)
SLOT_OF = {1: 0, 3: 1, 2: 2}


def dot(a, b, dims=NN):
    return lax.dot_general(a, b, dims, preferred_element_type=jnp.float32)


def one_hot(cond):
    return cond.astype(jnp.float32).astype(jnp.bfloat16)


def iota(shape, dim):
    return lax.broadcasted_iota(jnp.int32, shape, dim)


def permutation(shape):
    i, j = iota(shape, 0), iota(shape, 1)
    k, q, r = lax.div(lax.rem(j, 16), 4), lax.div(j, 16), lax.rem(j, 4)
    return one_hot(i == k * RANK + q * 4 + r)


def main_kernel(
    lang, live, lang_row, tokens, grad, weight, adown, aup,
    ig, gg,
    wbuf, wl, tok, og, adv, auv, su, sd, uu, dd, spd, spu, r1d, r1u, r2d, r2u, xout, xin, gv, igv, b2, btp, htp, pick,
    in_sem, y_s, y_r, a_s, a_r, b_s, b_r, f_s, f_r, c_s, c_r, t_s, t_r, tf_s, tf_r, tc_s, tc_r,
    u_s, u_r, d_s, d_r, pd_s, pd_r, pu_s, pu_r, xd_s, xd_r, xu_s, xu_r, xc_s, xc_r, g_s, g_r, e_s, e_r, own_s, out_s,
):
    f, e, o = lax.axis_index("fsdp"), lax.axis_index("dp"), lax.axis_index("owner")
    q, c = lax.div(e, 2), lax.rem(e, 2)
    x, zl = lax.rem(q, 4), lax.div(q, 4)
    z = o * 2 + zl
    pa = x * (1 - c) + z * c
    pb = z * (1 - c) + x * c

    def mod(v, n):
        return lax.rem(v + n, n)

    def at_ab(da, db):
        a, b = mod(pa + da, 4), mod(pb + db, 4)
        xx, zz = a * (1 - c) + b * c, b * (1 - c) + a * c
        return (f, lax.rem(zz, 2) * 8 + xx * 2 + c, lax.div(zz, 2))

    def at_y(s):
        return (mod(f + s, 4), e, o)

    def at_chip(chip):
        return (f, chip * 2 + c, o)

    def chip_of(dz, s):
        return lax.rem(zl + dz, 2) * 4 + mod(x - s, 4)

    other = (f, q * 2 + 1 - c, o)

    def rcopy(src, dst, ssem, rsem, dev):
        return pltpu.make_async_remote_copy(
            src_ref=src, dst_ref=dst, send_sem=ssem, recv_sem=rsem, device_id=dev, device_id_type=MESH
        )

    def await_ref(ref, sem):
        pltpu.make_async_copy(ref, ref, sem).wait()

    sends = []

    def send(*args):
        cp = rcopy(*args)
        cp.start()
        sends.append(cp)

    loads = [
        pltpu.make_async_copy(s, d, in_sem.at[i])
        for i, (s, d) in enumerate(((aup, auv), (adown, adv), (grad, og), (tokens, tok), (weight, wl)))
    ]
    for cp in loads:
        cp.start()

    barrier = pltpu.get_barrier_semaphore()
    peers = [at_y(s) for s in (1, 2, 3)]
    peers += [at_ab(s, 0) for s in (1, 2, 3)] + [at_ab(0, 1), at_ab(0, -1)]
    peers += [at_chip(lax.rem(q + s, CHIPS)) for s in range(1, CHIPS)] + [other]
    for dev in peers:
        pl.semaphore_signal(barrier, inc=1, device_id=dev, device_id_type=MESH)
    pl.semaphore_wait(barrier, len(peers))

    def piece(ref, slots, a, b):
        rows = pl.ds(pl.multiple_of(c * HALF + b * SUB, 16), SUB)
        cols = pl.ds(pl.multiple_of(a * (Q_ALL // 4), TILE), Q_ALL // 4)
        return ref.at[rows, cols] if slots is None else ref.at[slots, rows, cols]

    for s in (1, 3, 2):
        i = SLOT_OF[4 - s]
        send(piece(weight, None, pa, pb), piece(wbuf, i, pa, pb), y_s.at[s - 1], y_r.at[i], at_y(s))

    def choose(table, s, out):
        first = ((mod(f + s, 4) * 16 + e) * 2 + o) * TILES
        for k in range(TILES):
            out[pl.ds(k * RANK, RANK), :] = table[lax.rem(lang[first + k], LANGS)]

    loads[0].wait()
    for s in (2, 1, 3):
        choose(auv, s, su.at[s - 1])
        send(su.at[s - 1], uu.at[f], u_s.at[s - 1], u_r.at[s - 1], at_y(s))
    choose(auv, 0, uu.at[f])
    loads[2].wait()
    own = ((f * 16 + e) * 2 + o) * TILES
    slot = iota((TILE, Q_ALL), 0)
    for k in range(TILES):
        rows = pl.ds(k * TILE, TILE)
        og[rows, :] = jnp.where(slot < live[own + k], og[rows, :].astype(jnp.float32), 0.0).astype(jnp.bfloat16)

    groups = ((pl.ds(0, 2), (0, 1)), (pl.ds(2, 1), (2,)))

    def b_sends(s, g):
        unit = piece(wbuf, groups[g][0], mod(pa - s, 4), pb)
        send(unit, unit, b_s.at[0, s, g], b_r.at[0, s, g], at_ab(0, 1))
        send(unit, unit, b_s.at[1, s, g], b_r.at[1, s, g], at_ab(0, -1))

    for g in range(2):
        for i in groups[g][1]:
            await_ref(piece(wbuf, i, pa, pb), y_r.at[i])
        unit = piece(wbuf, groups[g][0], pa, pb)
        for s in (2, 1, 3):
            send(unit, unit, a_s.at[s - 1, g], a_r.at[s - 1, g], at_ab(s, 0))
        b_sends(0, g)

    n = iota((T, T), 1)
    chip, y, k = lax.div(n, 64), lax.rem(lax.div(n, 16), 4), lax.rem(lax.div(n, 4), 4)
    source = one_hot(iota((T, T), 0) == ((y * 16 + chip * 2 + c) * 2 + o) * TILES + k)
    langs = jnp.broadcast_to(lang_row[...].astype(jnp.float32), (16, T)).astype(jnp.bfloat16)
    langs = dot(langs, source)[:1]
    m, n = iota((ROWS, T), 0), iota((ROWS, T), 1)
    wanted = (lax.div(m, 4) + o * LANGS).astype(jnp.float32)
    pick[...] = one_hot((langs == wanted) & (lax.rem(n, 4) == lax.rem(m, 4)))

    j, t = iota((ROWS, T), 0), iota((ROWS, T), 1)
    limit = jnp.where(
        t < 2 * TILE,
        jnp.where(t < TILE, live[own], live[own + 1]),
        jnp.where(t < 3 * TILE, live[own + 2], live[own + 3]),
    )
    mask = (lax.div(j, RANK) == lax.div(t, TILE)) & (lax.rem(t, TILE) < limit)
    perm_t = permutation((ROWS, ROWS)).astype(jnp.float32).T.astype(jnp.bfloat16)

    def rows_by_chip(v):
        v = jnp.where(mask, v, 0.0).astype(jnp.bfloat16)
        return dot(perm_t, v).astype(jnp.bfloat16)

    for s in (1, 3, 2):
        await_ref(uu.at[mod(f - s, 4)], u_r.at[s - 1])
    loads[1].wait()
    for s in (2, 1, 3):
        choose(adv, s, sd.at[s - 1])
        send(sd.at[s - 1], dd.at[f], d_s.at[s - 1], d_r.at[s - 1], at_y(s))
    choose(adv, 0, dd.at[f])
    bt = jnp.zeros((ROWS, T), jnp.float32)
    bb = jnp.zeros((T, ROWS), jnp.float32)
    for y in range(YN):
        bt += dot(uu[y], og[:, y * Q_SH : (y + 1) * Q_SH], NT)
        bb += dot(og[:, y * Q_SH : (y + 1) * Q_SH], uu[y], NT)
    tt, jj = iota((T, ROWS), 0), iota((T, ROWS), 1)
    bb = jnp.where(lax.div(jj, RANK) == lax.div(tt, TILE), bb, 0.0).astype(jnp.bfloat16)
    b2[...] = (bb.astype(jnp.float32) * 2.0).astype(jnp.bfloat16)
    btp[...] = rows_by_chip(bt)

    loads[3].wait()
    for s in (2, 1, 3, 0):
        y = mod(f + s, 4)
        part = dot(btp[...], tok[:, pl.ds(pl.multiple_of(y * D_SH, TILE), D_SH)]).astype(jnp.bfloat16)
        if s:
            spd[s - 1] = part
            send(spd.at[s - 1], r1d.at[f], pd_s.at[s - 1], pd_r.at[s - 1], at_y(s))
        else:
            r1d[f] = part

    def spread(r1, r2, s, ssem, rsem):
        y = mod(f - s, 4)

        def one(i, _):
            chip = lax.rem(q + i, CHIPS)
            rcopy(
                r1.at[y, pl.ds(pl.multiple_of(chip * 16, 16), 16)], r2.at[q, y],
                ssem.at[s, i - 1], rsem, at_chip(chip),
            ).start()
            return 0

        lax.fori_loop(1, CHIPS, one, 0)
        pltpu.make_async_copy(r1.at[y, pl.ds(pl.multiple_of(q * 16, 16), 16)], r2.at[q, y], rsem).start()

    def spread_done(r1, r2, ssem):
        def one(i, _):
            rcopy(
                r1.at[0, pl.ds(0, 16)], r2.at[0, 0],
                ssem.at[lax.div(i, CHIPS - 1), lax.rem(i, CHIPS - 1)], ssem.at[0, 0], other,
            ).wait_send()
            return 0

        lax.fori_loop(0, YN * (CHIPS - 1), one, 0)

    spread(r1d, r2d, 0, xd_s, xd_r.at[0])

    for g in range(2):
        for s in (1, 3, 2):
            await_ref(piece(wbuf, groups[g][0], mod(pa - s, 4), pb), a_r.at[s - 1, g])
            b_sends(s, g)

    def block_to_other(rel):
        rows = pl.ds(pl.multiple_of(c * HALF + mod(pb + rel, 4) * SUB, 16), SUB)
        send(wbuf.at[:, rows], wbuf.at[:, rows], c_s.at[rel], c_r.at[rel], other)

    block_to_other(0)

    def pass_on(s, g):
        way = (1 - c) * (2 * lax.rem(z, 2) - 1) + c * (1 if s in (0, 2) else -1)
        unit = piece(wbuf, groups[g][0], mod(pa - s, 4), mod(pb - way, 4))
        await_ref(unit, b_r.at[lax.div(1 - way, 2), s, g])
        send(unit, unit, f_s.at[s, g], f_r.at[s, g], at_ab(0, way))

    def rest(s, g):
        way = (1 - c) * (2 * lax.rem(z, 2) - 1) + c * (1 if s in (0, 2) else -1)
        await_ref(piece(wbuf, groups[g][0], mod(pa - s, 4), mod(pb + way, 4)), b_r.at[lax.div(1 + way, 2), s, g])

    for g in range(2):
        pass_on(0, g)

    def columns(w, y, first, width):
        d = dd[y, :, pl.ds(first, width)]
        value = (dot(og[...], w, NT) + dot(b2[...], d)).astype(jnp.bfloat16)
        igv[:, pl.ds(pl.multiple_of(y * D_SH + first, TILE), width)] = value

    outs = []

    def emit(y, first, width):
        cols = pl.ds(pl.multiple_of(y * D_SH + first, TILE), width)
        cp = pltpu.make_async_copy(igv.at[:, cols], ig.at[:, cols], out_s.at[len(outs)])
        cp.start()
        outs.append(cp)

    loads[4].wait()

    def local_chunk(i, _):
        first = pl.multiple_of(i * LOCAL, TILE)
        columns(wl[pl.ds(first, LOCAL), :], f, first, LOCAL)
        return 0

    lax.fori_loop(0, D_SH // LOCAL, local_chunk, 0)
    emit(f, 0, D_SH)

    for s in (1, 3, 2):
        await_ref(dd.at[mod(f - s, 4)], d_r.at[s - 1])
    ht = jnp.zeros((ROWS, T), jnp.float32)
    for y in range(YN):
        ht += dot(dd[y], tok[:, y * D_SH : (y + 1) * D_SH], NT)
    htp[...] = rows_by_chip(ht)
    for s in (2, 1, 3, 0):
        y = mod(f + s, 4)
        part = dot(htp[...], og[:, pl.ds(pl.multiple_of(y * Q_SH, TILE), Q_SH)]).astype(jnp.bfloat16)
        if s:
            spu[s - 1] = part
            send(spu.at[s - 1], r1u.at[f], pu_s.at[s - 1], pu_r.at[s - 1], at_y(s))
        else:
            r1u[f] = part
    spread(r1u, r2u, 0, xu_s, xu_r.at[0])

    def gathered(i):
        y = mod(f + SLOTS[i], 4)
        for first, width in ((0, 512), (512, 2 * HALF - 512)):
            columns(wbuf[i, first : first + width, :], y, first, width)
        emit(y, 0, 2 * HALF)

    def spread_down(s):
        await_ref(r1d.at[mod(f - s, 4)], pd_r.at[s - 1])
        spread(r1d, r2d, s, xd_s, xd_r.at[0])

    def spread_up(s):
        await_ref(r1u.at[mod(f - s, 4)], pu_r.at[s - 1])
        spread(r1u, r2u, s, xu_s, xu_r.at[0])

    for g in range(2):
        for s in (1, 3, 2):
            pass_on(s, g)
    for g in range(2):
        for s in range(4):
            rest(s, g)
    for rel in (1, 3):
        block_to_other(rel)
    for s in (1, 3, 2):
        spread_down(s)
    for s in (1, 3, 2):
        spread_up(s)

    tail = pl.ds(pl.multiple_of(2 * HALF + c * MINE, 16), MINE)
    for s in (1, 3):
        i = SLOT_OF[4 - s]
        send(weight.at[tail], wbuf.at[i, tail], t_s.at[i], t_r.at[i], at_y(s))

    for g in range(2):
        for s in range(4):
            await_ref(piece(wbuf, groups[g][0], mod(pa - s, 4), mod(pb + 2, 4)), f_r.at[s, g])
    block_to_other(2)
    scale = 2.0 / 256.0
    late = G_ALL - CUT

    def send_sum(width):
        part, there = xout.at[:, pl.ds(0, width)], xin.at[:, pl.ds(0, width)]
        return rcopy(part, there, xc_s.at[0], xc_r.at[0], other)

    def start_gather(width, first):
        mine, place = gv.at[:, pl.ds(0, width)], gg.at[q, :, pl.ds(first, width)]
        for s in (2, 1, 3):
            rcopy(mine, place, g_s.at[s - 1], g_r.at[s - 1], at_chip(chip_of(0, -s))).start()
        rcopy(mine, place, g_s.at[3], g_r.at[3], at_chip(chip_of(1, 0))).start()
        rcopy(mine, place, e_s.at[0], e_r.at[0], other).start()
        pltpu.make_async_copy(mine, place, own_s.at[0]).start()

    await_ref(r2d, xd_r.at[0])
    down = dot(pick[...], r2d[...].reshape(T, D_SH))

    @pl.when(c == 0)
    def _():
        xout[:, : D_SH - CUT] = down[:, CUT:]
        await_ref(xin, xc_r.at[0])
        gv[...] = ((down[:, :CUT] + xin[...]) * scale).astype(jnp.bfloat16)
        start_gather(CUT, 0)

    @pl.when(c == 1)
    def _():
        xout[...] = down[:, :CUT]
        send_sum(CUT).start()

    await_ref(r2u, xu_r.at[0])
    up = dot(pick[...], r2u[...].reshape(T, Q_SH))

    @pl.when(c == 0)
    def _():
        xout[:, D_SH - CUT : late] = up
        send_sum(late).start()

    @pl.when(c == 1)
    def _():
        await_ref(xin.at[:, pl.ds(0, late)], xc_r.at[0])
        gv[:, : D_SH - CUT] = ((down[:, CUT:] + xin[:, : D_SH - CUT]) * scale).astype(jnp.bfloat16)
        gv[:, D_SH - CUT : late] = ((up + xin[:, D_SH - CUT : late]) * scale).astype(jnp.bfloat16)
        start_gather(late, CUT)

    for rel in range(4):
        rows = pl.ds(pl.multiple_of((1 - c) * HALF + mod(pa + rel, 4) * SUB, 16), SUB)
        await_ref(wbuf.at[:, rows], c_r.at[rel])
    gathered(0)

    for i, s in ((1, 1), (0, 3)):
        await_ref(wbuf.at[i, tail], t_r.at[i])
        rows = pl.ds(pl.multiple_of(2 * HALF + c * MINE + (1 - i) * (MINE // 2), 16), MINE // 2)
        send(wbuf.at[i, rows], wbuf.at[2, rows], tf_s.at[i], tf_r.at[i], at_y(s))
    near = wbuf.at[pl.ds(0, 2), tail]
    send(near, near, tc_s.at[0], tc_r.at[0], other)

    def place(dz, s, width, first):
        return gg.at[chip_of(dz, s), :, pl.ds(first, width)]

    def hand_over(width, first, dz, s):
        part = place(dz, s, width, first)
        await_ref(part, g_r.at[s - 1 if dz == 0 else 3 + s])
        rcopy(part, part, e_s.at[dz * 4 + s], e_r.at[dz * 4 + s], other).start()
        return part

    @pl.when(c == 0)
    def _():
        for s in (1, 3, 2):
            part = hand_over(CUT, 0, 0, s)
            rcopy(part, part, g_s.at[3 + s], g_r.at[3 + s], at_chip(chip_of(1, 0))).start()

    @pl.when(c == 1)
    def _():
        part = hand_over(late, CUT, 1, 0)
        for s in (2, 1, 3):
            rcopy(part, part, g_s.at[3 + s], g_r.at[3 + s], at_chip(chip_of(0, -s))).start()

    gathered(1)
    gathered(2)

    theirs = pl.ds(pl.multiple_of(2 * HALF + (1 - c) * MINE, 16), MINE)
    await_ref(wbuf.at[pl.ds(0, 2), theirs], tc_r.at[0])

    def last(i):
        y = mod(f + SLOTS[i], 4)
        columns(wbuf[i, 2 * HALF :, :], y, 2 * HALF, TAIL)
        emit(y, 2 * HALF, TAIL)

    last(0)
    last(1)
    for i in range(2):
        rows = pl.ds(pl.multiple_of(2 * HALF + c * MINE + (1 - i) * (MINE // 2), 16), MINE // 2)
        await_ref(wbuf.at[2, rows], tf_r.at[i])
    far = wbuf.at[2, tail]
    send(far, far, tc_s.at[1], tc_r.at[1], other)

    @pl.when(c == 0)
    def _():
        for s in (0, 1, 3, 2):
            hand_over(CUT, 0, 1, s)

    @pl.when(c == 1)
    def _():
        for dz in (0, 1):
            for s in (1, 3, 2):
                hand_over(late, CUT, dz, s)

    await_ref(wbuf.at[2, theirs], tc_r.at[1])
    last(2)

    def finish(width, first, theirs_width, theirs_first):
        for dz in (0, 1):
            for s in range(4):
                await_ref(place(dz, s, theirs_width, theirs_first), e_r.at[dz * 4 + s])
        mine = gv.at[:, pl.ds(0, width)]
        await_ref(mine, own_s.at[0])
        for i in range(7):
            rcopy(mine, place(0, 0, width, first), g_s.at[i], g_r.at[i], other).wait_send()
        for i in range(8):
            rcopy(mine, place(0, 0, width, first), e_s.at[i], e_r.at[i], other).wait_send()

    @pl.when(c == 0)
    def _():
        send_sum(late).wait_send()
        finish(CUT, 0, late, CUT)

    @pl.when(c == 1)
    def _():
        send_sum(CUT).wait_send()
        finish(late, CUT, CUT, 0)

    for cp in sends:
        cp.wait_send()
    spread_done(r1d, r2d, xd_s)
    spread_done(r1u, r2u, xu_s)
    for cp in outs:
        cp.wait()


def finish_kernel(gg, ig_in, down, up, ig, buf, dv, uv, iv, in_s, out_s):
    loads, through = [], []
    for g in range(4):
        part, rows = pl.ds(g * 32, 32), pl.ds(g * TILE, TILE)
        loads.append(pltpu.make_async_copy(gg.at[:, part], buf.at[:, part], in_s.at[0, g]))
        through.append(pltpu.make_async_copy(ig_in.at[rows], iv.at[rows], in_s.at[1, g]))
        loads[-1].start()
        through[-1].start()
    perm = permutation((ROWS, ROWS))
    outs = []
    for g in range(4):
        loads[g].wait()
        for h in (2 * g, 2 * g + 1):
            rows = buf[:, h * 16 : (h + 1) * 16, :].reshape(ROWS, G_ALL)
            rows = dot(perm, rows).astype(jnp.bfloat16).reshape(4, RANK, G_ALL)
            dv[h * 4 : (h + 1) * 4] = rows[:, :, :D_SH]
            uv[h * 4 : (h + 1) * 4] = rows[:, :, D_SH:]
        for i, (src, dst) in enumerate(((dv, down), (uv, up))):
            cp = pltpu.make_async_copy(src.at[g * 8 : (g + 1) * 8], dst.at[g * 8 : (g + 1) * 8], out_s.at[i, g])
            cp.start()
            outs.append(cp)
        through[g].wait()
        rows = pl.ds(g * TILE, TILE)
        cp = pltpu.make_async_copy(iv.at[rows], ig.at[rows], out_s.at[2, g])
        cp.start()
        outs.append(cp)
    for cp in outs:
        cp.wait()


def on_device(tokens, output_gradient, tile_language, tile_live_count, frozen_weight, adapter_down, adapter_up):
    bf = jnp.bfloat16
    hbm, smem, vmem = (pl.BlockSpec(memory_space=s) for s in (pl.ANY, pltpu.SMEM, pltpu.VMEM))
    sem = pltpu.SemaphoreType.DMA

    def sems(*shapes):
        return [sem(s) for s in shapes]

    def buf(*shape, dtype=bf):
        return pltpu.VMEM(shape, dtype)

    ig, gg = pl.pallas_call(
        main_kernel,
        out_shape=(
            jax.ShapeDtypeStruct((T, D_ALL), bf),
            jax.ShapeDtypeStruct((CHIPS, ROWS, G_ALL), bf),
        ),
        in_specs=[smem, smem, vmem, hbm, hbm, hbm, hbm, hbm],
        out_specs=(hbm, hbm),
        scratch_shapes=[
            buf(3, D_SH, Q_ALL),
            buf(D_SH, Q_ALL),
            buf(T, D_ALL),
            buf(T, Q_ALL),
            buf(LANGS, RANK, D_SH),
            buf(LANGS, RANK, Q_SH),
            buf(3, ROWS, Q_SH),
            buf(3, ROWS, D_SH),
            buf(YN, ROWS, Q_SH),
            buf(YN, ROWS, D_SH),
            buf(3, ROWS, D_SH),
            buf(3, ROWS, Q_SH),
            buf(YN, ROWS, D_SH),
            buf(YN, ROWS, Q_SH),
            buf(CHIPS, YN, 16, D_SH),
            buf(CHIPS, YN, 16, Q_SH),
            buf(ROWS, CUT, dtype=jnp.float32),
            buf(ROWS, CUT, dtype=jnp.float32),
            buf(ROWS, CUT),
            buf(T, D_ALL),
            buf(T, ROWS),
            buf(ROWS, T),
            buf(ROWS, T),
            buf(ROWS, T),
            *sems((5,), (3,), (3,), (3, 2), (3, 2), (2, 4, 2), (2, 4, 2), (4, 2), (4, 2), (4,), (4,)),
            *sems((2,), (2,), (2,), (2,), (2,), (2,)),
            *sems((3,), (3,), (3,), (3,), (3,), (3,), (3,), (3,), (4, 7), (1,), (4, 7), (1,)),
            *sems((1,), (1,), (7,), (7,), (8,), (8,), (1,), (7,)),
        ],
        compiler_params=pltpu.CompilerParams(
            collective_id=0, has_side_effects=True, vmem_limit_bytes=58 * 2**20
        ),
        cost_estimate=pl.CostEstimate(flops=12 * 10**9, bytes_accessed=40 * 10**6, transcendentals=0),
        name="exchange",
    )(
        tile_language, tile_live_count, tile_language.reshape(1, T),
        tokens, output_gradient, frozen_weight, adapter_down, adapter_up,
    )
    down, up, ig = pl.pallas_call(
        finish_kernel,
        out_shape=(
            jax.ShapeDtypeStruct((LANGS, RANK, D_SH), bf),
            jax.ShapeDtypeStruct((LANGS, RANK, Q_SH), bf),
            jax.ShapeDtypeStruct((T, D_ALL), bf),
        ),
        in_specs=[hbm, hbm],
        out_specs=(hbm, hbm, hbm),
        scratch_shapes=[
            buf(CHIPS, ROWS, G_ALL), buf(LANGS, RANK, D_SH), buf(LANGS, RANK, Q_SH), buf(T, D_ALL),
            *sems((2, 4), (3, 4)),
        ],
        compiler_params=pltpu.CompilerParams(vmem_limit_bytes=60 * 2**20),
        name="finish",
    )(gg, ig)
    return ig, down, up


def solution(mesh):
    tok = P(("fsdp", "dp", "owner"), None)
    adapter = P("owner", None, "fsdp")
    return jax.shard_map(
        on_device,
        mesh=mesh,
        in_specs=(tok, tok, P(), P(), P("fsdp", None), adapter, adapter),
        out_specs=(tok, adapter, adapter),
        check_vma=False,
    )
```

time: 115 us -> 98 us (0.85)
  the two profiles are of different devices: /device:TPU:57 before, /device:TPU:1 now
where the time goes in v2:
time: 98 us; the launch traced here: 97.8 us
  Pallas kernels  97 us (99%)
    pallas_call x1, Pallas kernels, on_device(): pl.pallas_call(main_kernel, out_shape=(jax.ShapeDtypeStruct((T, D_ALL), b...  90.4 us
    pallas_call x1, Pallas kernels, on_device(): pl.pallas_call(finish_kernel, out_shape=(jax.ShapeDtypeStruct((LANGS, RAN...  6.68 us

profile of v2, /device:TPU:1, one launch (start us, length us, event | category | flops | bytes accessed | tf_op | source)
XLA Modules:
  0.0 97.8 jit_solution(3402949464597865063)
XLA Ops:
  0.6 90.4 %exchange.1 = (bf16[512,4608]{1,0:T(8,128)(2,1)}, bf16[8,128,1664]{2,1,0:T(8,128)(2,1)}) custom-call(s32[512]{0:T(512)} %lang.1, s32[512]{0:T(512)} %live.1, s32[1,512]{1,0:T(1,128)} %bitcast.1, bf16[512,4608]{1,0:T(8,128)(2,1)} %tokens.1, bf16[512,2048]{1,0:T(8,128)(2,1)} %grad.1, bf16[1152,2048]{1,0:T(8,128)(2,1)} %weight.1, bf16[32,32,1152]{2,1,0:T(8,128)(2,1)} %adown.1, ...), custom_call_target="tpu_custom_call" | custom-call | flops 12000000000 | bytes 40000000 | tf_op jit(solution)/shard_map/exchange/pallas_call | solution.py:512
  91.0 6.7 %finish.1 = (bf16[32,32,1152]{2,1,0:T(8,128)(2,1)}, bf16[32,32,512]{2,1,0:T(8,128)(2,1)}, bf16[512,4608]{1,0:T(8,128)(2,1)}) custom-call(bf16[8,128,1664]{2,1,0:T(8,128)(2,1)} %get-tuple-element.8.gg, bf16[512,4608]{1,0:T(8,128)(2,1)} %get-tuple-element.9.ig_in), custom_call_target="tpu_custom_call" | custom-call | tf_op jit(solution)/shard_map/finish/pallas_call | solution.py:559

commit v3 on v2

--- a/solution.py
+++ b/solution.py
@@ -22,7 +22,6 @@
 D_ALL, Q_ALL = 4608, 2048
 D_SH, Q_SH = D_ALL // YN, Q_ALL // YN
 G_ALL = D_SH + Q_SH
-CUT = 896
 SUB = 112
 HALF = 4 * SUB
 TAIL = D_SH - 2 * HALF
@@ -30,6 +29,7 @@
 LOCAL = 384
 SLOTS = (1, 3, 2)
 SLOT_OF = {1: 0, 3: 1, 2: 2}
+PARTS = ((0, 640), (640, 512), (D_SH, Q_SH))
 
 
 def dot(a, b, dims=NN):
@@ -53,9 +53,9 @@
 def main_kernel(
     lang, live, lang_row, tokens, grad, weight, adown, aup,
     ig, gg,
-    wbuf, wl, tok, og, adv, auv, su, sd, uu, dd, spd, spu, r1d, r1u, r2d, r2u, xout, xin, gv, igv, b2, btp, htp, pick,
+    wbuf, wl, tok, og, adv, auv, su, sd, uu, dd, spd, spu, r1d, r1u, r2d, r2u, xout, xin, gv, b2, btp, htp, pick,
     in_sem, y_s, y_r, a_s, a_r, b_s, b_r, f_s, f_r, c_s, c_r, t_s, t_r, tf_s, tf_r, tc_s, tc_r,
-    u_s, u_r, d_s, d_r, pd_s, pd_r, pu_s, pu_r, xd_s, xd_r, xu_s, xu_r, xc_s, xc_r, g_s, g_r, e_s, e_r, own_s, out_s,
+    u_s, u_r, d_s, d_r, pd_s, pd_r, pu_s, pu_r, xd_s, xd_r, xu_s, xu_r, xc_s, xc_r, g_s, g_r, e_s, e_r, own_s,
 ):
     f, e, o = lax.axis_index("fsdp"), lax.axis_index("dp"), lax.axis_index("owner")
     q, c = lax.div(e, 2), lax.rem(e, 2)
@@ -127,11 +127,6 @@
         for k in range(TILES):
             out[pl.ds(k * RANK, RANK), :] = table[lax.rem(lang[first + k], LANGS)]
 
-    loads[0].wait()
-    for s in (2, 1, 3):
-        choose(auv, s, su.at[s - 1])
-        send(su.at[s - 1], uu.at[f], u_s.at[s - 1], u_r.at[s - 1], at_y(s))
-    choose(auv, 0, uu.at[f])
     loads[2].wait()
     own = ((f * 16 + e) * 2 + o) * TILES
     slot = iota((TILE, Q_ALL), 0)
@@ -152,8 +147,13 @@
         unit = piece(wbuf, groups[g][0], pa, pb)
         for s in (2, 1, 3):
             send(unit, unit, a_s.at[s - 1, g], a_r.at[s - 1, g], at_ab(s, 0))
-        b_sends(0, g)
-
+        if g == 0:
+            loads[0].wait()
+            for s in (2, 1, 3):
+                choose(auv, s, su.at[s - 1])
+                send(su.at[s - 1], uu.at[f], u_s.at[s - 1], u_r.at[s - 1], at_y(s))
+
+    choose(auv, 0, uu.at[f])
     n = iota((T, T), 1)
     chip, y, k = lax.div(n, 64), lax.rem(lax.div(n, 16), 4), lax.rem(lax.div(n, 4), 4)
     source = one_hot(iota((T, T), 0) == ((y * 16 + chip * 2 + c) * 2 + o) * TILES + k)
@@ -178,11 +178,8 @@
 
     for s in (1, 3, 2):
         await_ref(uu.at[mod(f - s, 4)], u_r.at[s - 1])
-    loads[1].wait()
-    for s in (2, 1, 3):
-        choose(adv, s, sd.at[s - 1])
-        send(sd.at[s - 1], dd.at[f], d_s.at[s - 1], d_r.at[s - 1], at_y(s))
-    choose(adv, 0, dd.at[f])
+    for g in range(2):
+        b_sends(0, g)
     bt = jnp.zeros((ROWS, T), jnp.float32)
     bb = jnp.zeros((T, ROWS), jnp.float32)
     for y in range(YN):
@@ -203,6 +200,12 @@
         else:
             r1d[f] = part
 
+    loads[1].wait()
+    for s in (2, 1, 3):
+        choose(adv, s, sd.at[s - 1])
+        send(sd.at[s - 1], dd.at[f], d_s.at[s - 1], d_r.at[s - 1], at_y(s))
+    choose(adv, 0, dd.at[f])
+
     def spread(r1, r2, s, ssem, rsem):
         y = mod(f - s, 4)
 
@@ -256,15 +259,7 @@
     def columns(w, y, first, width):
         d = dd[y, :, pl.ds(first, width)]
         value = (dot(og[...], w, NT) + dot(b2[...], d)).astype(jnp.bfloat16)
-        igv[:, pl.ds(pl.multiple_of(y * D_SH + first, TILE), width)] = value
-
-    outs = []
-
-    def emit(y, first, width):
-        cols = pl.ds(pl.multiple_of(y * D_SH + first, TILE), width)
-        cp = pltpu.make_async_copy(igv.at[:, cols], ig.at[:, cols], out_s.at[len(outs)])
-        cp.start()
-        outs.append(cp)
+        ig[:, pl.ds(pl.multiple_of(y * D_SH + first, TILE), width)] = value
 
     loads[4].wait()
 
@@ -274,8 +269,30 @@
         return 0
 
     lax.fori_loop(0, D_SH // LOCAL, local_chunk, 0)
-    emit(f, 0, D_SH)
-
+
+    def gathered(i):
+        y = mod(f + SLOTS[i], 4)
+        for first, width in ((0, 512), (512, 2 * HALF - 512)):
+            columns(wbuf[i, first : first + width, :], y, first, width)
+
+    def spread_down(s):
+        await_ref(r1d.at[mod(f - s, 4)], pd_r.at[s - 1])
+        spread(r1d, r2d, s, xd_s, xd_r.at[0])
+
+    def spread_up(s):
+        await_ref(r1u.at[mod(f - s, 4)], pu_r.at[s - 1])
+        spread(r1u, r2u, s, xu_s, xu_r.at[0])
+
+    for s in (1, 3, 2):
+        spread_down(s)
+    for g in range(2):
+        for s in (1, 3, 2):
+            pass_on(s, g)
+    for g in range(2):
+        for s in range(4):
+            rest(s, g)
+    for rel in (1, 3):
+        block_to_other(rel)
     for s in (1, 3, 2):
         await_ref(dd.at[mod(f - s, 4)], d_r.at[s - 1])
     ht = jnp.zeros((ROWS, T), jnp.float32)
@@ -292,33 +309,6 @@
             r1u[f] = part
     spread(r1u, r2u, 0, xu_s, xu_r.at[0])
 
-    def gathered(i):
-        y = mod(f + SLOTS[i], 4)
-        for first, width in ((0, 512), (512, 2 * HALF - 512)):
-            columns(wbuf[i, first : first + width, :], y, first, width)
-        emit(y, 0, 2 * HALF)
-
-    def spread_down(s):
-        await_ref(r1d.at[mod(f - s, 4)], pd_r.at[s - 1])
-        spread(r1d, r2d, s, xd_s, xd_r.at[0])
-
-    def spread_up(s):
-        await_ref(r1u.at[mod(f - s, 4)], pu_r.at[s - 1])
-        spread(r1u, r2u, s, xu_s, xu_r.at[0])
-
-    for g in range(2):
-        for s in (1, 3, 2):
-            pass_on(s, g)
-    for g in range(2):
-        for s in range(4):
-            rest(s, g)
-    for rel in (1, 3):
-        block_to_other(rel)
-    for s in (1, 3, 2):
-        spread_down(s)
-    for s in (1, 3, 2):
-        spread_up(s)
-
     tail = pl.ds(pl.multiple_of(2 * HALF + c * MINE, 16), MINE)
     for s in (1, 3):
         i = SLOT_OF[4 - s]
@@ -328,55 +318,84 @@
         for s in range(4):
             await_ref(piece(wbuf, groups[g][0], mod(pa - s, 4), mod(pb + 2, 4)), f_r.at[s, g])
     block_to_other(2)
+
     scale = 2.0 / 256.0
-    late = G_ALL - CUT
 
     def send_sum(width):
         part, there = xout.at[:, pl.ds(0, width)], xin.at[:, pl.ds(0, width)]
         return rcopy(part, there, xc_s.at[0], xc_r.at[0], other)
 
-    def start_gather(width, first):
-        mine, place = gv.at[:, pl.ds(0, width)], gg.at[q, :, pl.ds(first, width)]
+    def place(dz, s, r):
+        return gg.at[chip_of(dz, s), :, pl.ds(*PARTS[r])]
+
+    def mine(r):
+        return gv.at[:, pl.ds(PARTS[r][0] % D_SH, PARTS[r][1])]
+
+    def to_x(src, dst, r, k):
         for s in (2, 1, 3):
-            rcopy(mine, place, g_s.at[s - 1], g_r.at[s - 1], at_chip(chip_of(0, -s))).start()
-        rcopy(mine, place, g_s.at[3], g_r.at[3], at_chip(chip_of(1, 0))).start()
-        rcopy(mine, place, e_s.at[0], e_r.at[0], other).start()
-        pltpu.make_async_copy(mine, place, own_s.at[0]).start()
+            rcopy(src, dst, g_s.at[r % 2, k + s - 1], g_r.at[r % 2, k + s - 1], at_chip(chip_of(0, -s))).start()
+
+    def to_z(src, dst, r, k):
+        rcopy(src, dst, g_s.at[r % 2, k], g_r.at[r % 2, k], at_chip(chip_of(1, 0))).start()
+
+    def to_core(src, dst, r, k):
+        rcopy(src, dst, e_s.at[r % 2, k], e_r.at[r % 2, k], other).start()
+
+    def hand_over(dz, s, r):
+        part = place(dz, s, r)
+        await_ref(part, g_r.at[r % 2, s - 1 if dz == 0 else 3 + s])
+        to_core(part, part, r, dz * 4 + s)
+        return part
 
     await_ref(r2d, xd_r.at[0])
     down = dot(pick[...], r2d[...].reshape(T, D_SH))
 
+    @pl.when(c == 1)
+    def _():
+        xout[...] = down
+        send_sum(D_SH).start()
+
+    for s in (1, 3, 2):
+        spread_up(s)
+
     @pl.when(c == 0)
     def _():
-        xout[:, : D_SH - CUT] = down[:, CUT:]
         await_ref(xin, xc_r.at[0])
-        gv[...] = ((down[:, :CUT] + xin[...]) * scale).astype(jnp.bfloat16)
-        start_gather(CUT, 0)
-
-    @pl.when(c == 1)
-    def _():
-        xout[...] = down[:, :CUT]
-        send_sum(CUT).start()
-
-    await_ref(r2u, xu_r.at[0])
-    up = dot(pick[...], r2u[...].reshape(T, Q_SH))
-
-    @pl.when(c == 0)
-    def _():
-        xout[:, D_SH - CUT : late] = up
-        send_sum(late).start()
-
-    @pl.when(c == 1)
-    def _():
-        await_ref(xin.at[:, pl.ds(0, late)], xc_r.at[0])
-        gv[:, : D_SH - CUT] = ((down[:, CUT:] + xin[:, : D_SH - CUT]) * scale).astype(jnp.bfloat16)
-        gv[:, D_SH - CUT : late] = ((up + xin[:, D_SH - CUT : late]) * scale).astype(jnp.bfloat16)
-        start_gather(late, CUT)
+        gv[...] = ((down + xin[...]) * scale).astype(jnp.bfloat16)
+        to_z(mine(1), place(0, 0, 1), 1, 3)
+        to_x(mine(0), place(0, 0, 0), 0, 0)
+        to_x(mine(1), place(0, 0, 1), 1, 0)
+        to_z(mine(0), place(0, 0, 0), 0, 3)
+        for r in (0, 1):
+            to_core(mine(r), place(0, 0, r), r, 0)
+            pltpu.make_async_copy(mine(r), place(0, 0, r), own_s.at[r]).start()
 
     for rel in range(4):
         rows = pl.ds(pl.multiple_of((1 - c) * HALF + mod(pa + rel, 4) * SUB, 16), SUB)
         await_ref(wbuf.at[:, rows], c_r.at[rel])
     gathered(0)
+
+    await_ref(r2u, xu_r.at[0])
+    up = dot(pick[...], r2u[...].reshape(T, Q_SH))
+
+    @pl.when(c == 0)
+    def _():
+        xout[:, :Q_SH] = up
+        send_sum(Q_SH).start()
+        part = hand_over(1, 0, 1)
+        to_x(part, part, 1, 4)
+        for s in (1, 3, 2):
+            part = hand_over(0, s, 0)
+            to_z(part, part, 0, 3 + s)
+
+    @pl.when(c == 1)
+    def _():
+        await_ref(xin.at[:, pl.ds(0, Q_SH)], xc_r.at[0])
+        gv[:, :Q_SH] = ((up + xin[:, :Q_SH]) * scale).astype(jnp.bfloat16)
+        to_z(mine(2), place(0, 0, 2), 2, 3)
+        to_x(mine(2), place(0, 0, 2), 2, 0)
+        to_core(mine(2), place(0, 0, 2), 2, 0)
+        pltpu.make_async_copy(mine(2), place(0, 0, 2), own_s.at[0]).start()
 
     for i, s in ((1, 1), (0, 3)):
         await_ref(wbuf.at[i, tail], t_r.at[i])
@@ -385,40 +404,22 @@
     near = wbuf.at[pl.ds(0, 2), tail]
     send(near, near, tc_s.at[0], tc_r.at[0], other)
 
-    def place(dz, s, width, first):
-        return gg.at[chip_of(dz, s), :, pl.ds(first, width)]
-
-    def hand_over(width, first, dz, s):
-        part = place(dz, s, width, first)
-        await_ref(part, g_r.at[s - 1 if dz == 0 else 3 + s])
-        rcopy(part, part, e_s.at[dz * 4 + s], e_r.at[dz * 4 + s], other).start()
-        return part
-
-    @pl.when(c == 0)
-    def _():
-        for s in (1, 3, 2):
-            part = hand_over(CUT, 0, 0, s)
-            rcopy(part, part, g_s.at[3 + s], g_r.at[3 + s], at_chip(chip_of(1, 0))).start()
-
     @pl.when(c == 1)
     def _():
-        part = hand_over(late, CUT, 1, 0)
-        for s in (2, 1, 3):
-            rcopy(part, part, g_s.at[3 + s], g_r.at[3 + s], at_chip(chip_of(0, -s))).start()
+        part = hand_over(1, 0, 2)
+        to_x(part, part, 2, 4)
 
     gathered(1)
     gathered(2)
-
     theirs = pl.ds(pl.multiple_of(2 * HALF + (1 - c) * MINE, 16), MINE)
     await_ref(wbuf.at[pl.ds(0, 2), theirs], tc_r.at[0])
 
-    def last(i):
+    w = wbuf[0:2, 2 * HALF :, :].reshape(2 * TAIL, Q_ALL)
+    near_sum = dot(og[...], w, NT)
+    for i in range(2):
         y = mod(f + SLOTS[i], 4)
-        columns(wbuf[i, 2 * HALF :, :], y, 2 * HALF, TAIL)
-        emit(y, 2 * HALF, TAIL)
-
-    last(0)
-    last(1)
+        value = near_sum[:, i * TAIL : (i + 1) * TAIL] + dot(b2[...], dd[y, :, 2 * HALF :])
+        ig[:, pl.ds(pl.multiple_of(y * D_SH + 2 * HALF, TILE), TAIL)] = value.astype(jnp.bfloat16)
     for i in range(2):
         rows = pl.ds(pl.multiple_of(2 * HALF + c * MINE + (1 - i) * (MINE // 2), 16), MINE // 2)
         await_ref(wbuf.at[2, rows], tf_r.at[i])
@@ -427,79 +428,79 @@
 
     @pl.when(c == 0)
     def _():
-        for s in (0, 1, 3, 2):
-            hand_over(CUT, 0, 1, s)
-
-    @pl.when(c == 1)
-    def _():
         for dz in (0, 1):
             for s in (1, 3, 2):
-                hand_over(late, CUT, dz, s)
+                hand_over(dz, s, 1)
+        for s in (0, 1, 3, 2):
+            hand_over(1, s, 0)
+
+    @pl.when(c == 1)
+    def _():
+        for dz in (0, 1):
+            for s in (1, 3, 2):
+                hand_over(dz, s, 2)
 
     await_ref(wbuf.at[2, theirs], tc_r.at[1])
-    last(2)
-
-    def finish(width, first, theirs_width, theirs_first):
-        for dz in (0, 1):
-            for s in range(4):
-                await_ref(place(dz, s, theirs_width, theirs_first), e_r.at[dz * 4 + s])
-        mine = gv.at[:, pl.ds(0, width)]
-        await_ref(mine, own_s.at[0])
-        for i in range(7):
-            rcopy(mine, place(0, 0, width, first), g_s.at[i], g_r.at[i], other).wait_send()
-        for i in range(8):
-            rcopy(mine, place(0, 0, width, first), e_s.at[i], e_r.at[i], other).wait_send()
+    columns(wbuf[2, 2 * HALF :, :], mod(f + SLOTS[2], 4), 2 * HALF, TAIL)
+
+    def finish(ours, theirs, width):
+        for r in theirs:
+            for dz in (0, 1):
+                for s in range(4):
+                    await_ref(place(dz, s, r), e_r.at[r % 2, dz * 4 + s])
+        send_sum(width).wait_send()
+        for r in ours:
+            await_ref(mine(r), own_s.at[r % 2])
+            for k in range(7):
+                rcopy(mine(r), place(0, 0, r), g_s.at[r % 2, k], g_r.at[r % 2, k], other).wait_send()
+            for k in range(8):
+                rcopy(mine(r), place(0, 0, r), e_s.at[r % 2, k], e_r.at[r % 2, k], other).wait_send()
 
     @pl.when(c == 0)
     def _():
-        send_sum(late).wait_send()
-        finish(CUT, 0, late, CUT)
+        finish((0, 1), (2,), Q_SH)
 
     @pl.when(c == 1)
     def _():
-        send_sum(CUT).wait_send()
-        finish(late, CUT, CUT, 0)
+        finish((2,), (0, 1), D_SH)
 
     for cp in sends:
         cp.wait_send()
     spread_done(r1d, r2d, xd_s)
     spread_done(r1u, r2u, xu_s)
-    for cp in outs:
-        cp.wait()
-
-
-def finish_kernel(gg, ig_in, down, up, ig, buf, dv, uv, iv, in_s, out_s):
-    loads, through = [], []
+
+
+def finish_kernel(gg, ig_in, down, up, ig, dv, uv, out_s):
+    outs = []
+
+    def emit(src, dst, i, g):
+        cp = pltpu.make_async_copy(src, dst, out_s.at[i, g])
+        cp.start()
+        outs.append(cp)
+
     for g in range(4):
-        part, rows = pl.ds(g * 32, 32), pl.ds(g * TILE, TILE)
-        loads.append(pltpu.make_async_copy(gg.at[:, part], buf.at[:, part], in_s.at[0, g]))
-        through.append(pltpu.make_async_copy(ig_in.at[rows], iv.at[rows], in_s.at[1, g]))
-        loads[-1].start()
-        through[-1].start()
+        rows = pl.ds(g * TILE, TILE)
+        emit(ig_in.at[rows], ig.at[rows], 2, g)
     perm = permutation((ROWS, ROWS))
-    outs = []
     for g in range(4):
-        loads[g].wait()
         for h in (2 * g, 2 * g + 1):
-            rows = buf[:, h * 16 : (h + 1) * 16, :].reshape(ROWS, G_ALL)
+            rows = gg[:, h * 16 : (h + 1) * 16, :].reshape(ROWS, G_ALL)
             rows = dot(perm, rows).astype(jnp.bfloat16).reshape(4, RANK, G_ALL)
             dv[h * 4 : (h + 1) * 4] = rows[:, :, :D_SH]
             uv[h * 4 : (h + 1) * 4] = rows[:, :, D_SH:]
-        for i, (src, dst) in enumerate(((dv, down), (uv, up))):
-            cp = pltpu.make_async_copy(src.at[g * 8 : (g + 1) * 8], dst.at[g * 8 : (g + 1) * 8], out_s.at[i, g])
-            cp.start()
-            outs.append(cp)
-        through[g].wait()
-        rows = pl.ds(g * TILE, TILE)
-        cp = pltpu.make_async_copy(iv.at[rows], ig.at[rows], out_s.at[2, g])
-        cp.start()
-        outs.append(cp)
+        part = pl.ds(g * 8, 8)
+        emit(dv.at[part], down.at[part], 0, g)
+        emit(uv.at[part], up.at[part], 1, g)
     for cp in outs:
         cp.wait()
 
 
 def on_device(tokens, output_gradient, tile_language, tile_live_count, frozen_weight, adapter_down, adapter_up):
     bf = jnp.bfloat16
+    pin = pltpu.with_memory_space_constraint
+    tokens, output_gradient, frozen_weight, adapter_down, adapter_up = (
+        pin(a, pltpu.HBM) for a in (tokens, output_gradient, frozen_weight, adapter_down, adapter_up)
+    )
     hbm, smem, vmem = (pl.BlockSpec(memory_space=s) for s in (pl.ANY, pltpu.SMEM, pltpu.VMEM))
     sem = pltpu.SemaphoreType.DMA
 
@@ -512,11 +513,11 @@
     ig, gg = pl.pallas_call(
         main_kernel,
         out_shape=(
-            jax.ShapeDtypeStruct((T, D_ALL), bf),
-            jax.ShapeDtypeStruct((CHIPS, ROWS, G_ALL), bf),
+            buf(T, D_ALL),
+            buf(CHIPS, ROWS, G_ALL),
         ),
         in_specs=[smem, smem, vmem, hbm, hbm, hbm, hbm, hbm],
-        out_specs=(hbm, hbm),
+        out_specs=(vmem, vmem),
         scratch_shapes=[
             buf(3, D_SH, Q_ALL),
             buf(D_SH, Q_ALL),
@@ -534,10 +535,9 @@
             buf(YN, ROWS, Q_SH),
             buf(CHIPS, YN, 16, D_SH),
             buf(CHIPS, YN, 16, Q_SH),
-            buf(ROWS, CUT, dtype=jnp.float32),
-            buf(ROWS, CUT, dtype=jnp.float32),
-            buf(ROWS, CUT),
-            buf(T, D_ALL),
+            buf(ROWS, D_SH, dtype=jnp.float32),
+            buf(ROWS, D_SH, dtype=jnp.float32),
+            buf(ROWS, D_SH),
             buf(T, ROWS),
             buf(ROWS, T),
             buf(ROWS, T),
@@ -545,15 +545,15 @@
             *sems((5,), (3,), (3,), (3, 2), (3, 2), (2, 4, 2), (2, 4, 2), (4, 2), (4, 2), (4,), (4,)),
             *sems((2,), (2,), (2,), (2,), (2,), (2,)),
             *sems((3,), (3,), (3,), (3,), (3,), (3,), (3,), (3,), (4, 7), (1,), (4, 7), (1,)),
-            *sems((1,), (1,), (7,), (7,), (8,), (8,), (1,), (7,)),
+            *sems((1,), (1,), (2, 7), (2, 7), (2, 8), (2, 8), (2,)),
         ],
         compiler_params=pltpu.CompilerParams(
-            collective_id=0, has_side_effects=True, vmem_limit_bytes=58 * 2**20
+            collective_id=0, has_side_effects=True, vmem_limit_bytes=46 * 2**20
         ),
         cost_estimate=pl.CostEstimate(flops=12 * 10**9, bytes_accessed=40 * 10**6, transcendentals=0),
         name="exchange",
     )(
-        tile_language, tile_live_count, tile_language.reshape(1, T),
+        pin(tile_language, pltpu.HBM), pin(tile_live_count, pltpu.HBM), tile_language.reshape(1, T),
         tokens, output_gradient, frozen_weight, adapter_down, adapter_up,
     )
     down, up, ig = pl.pallas_call(
@@ -563,15 +563,12 @@
             jax.ShapeDtypeStruct((LANGS, RANK, Q_SH), bf),
             jax.ShapeDtypeStruct((T, D_ALL), bf),
         ),
-        in_specs=[hbm, hbm],
+        in_specs=[vmem, vmem],
         out_specs=(hbm, hbm, hbm),
-        scratch_shapes=[
-            buf(CHIPS, ROWS, G_ALL), buf(LANGS, RANK, D_SH), buf(LANGS, RANK, Q_SH), buf(T, D_ALL),
-            *sems((2, 4), (3, 4)),
-        ],
-        compiler_params=pltpu.CompilerParams(vmem_limit_bytes=60 * 2**20),
+        scratch_shapes=[buf(LANGS, RANK, D_SH), buf(LANGS, RANK, Q_SH), sem((3, 4))],
+        compiler_params=pltpu.CompilerParams(vmem_limit_bytes=16 * 2**20),
         name="finish",
-    )(gg, ig)
+    )(pin(gg, pltpu.VMEM), pin(ig, pltpu.VMEM))
     return ig, down, up
 
 

time: 98 us -> 91 us (0.929)
  Pallas kernels: 97 us -> 90 us
    pallas_call x1, Pallas kernels: 90.4 us -> 86.7 us  [on_device(): pl.pallas_call(main_kernel, out_shape=(buf(T, D_ALL), buf(CHIPS, ROWS, G_...]
    pallas_call x1, Pallas kernels: 6.68 us -> 3.32 us  [on_device(): pl.pallas_call(finish_kernel, out_shape=(jax.ShapeDtypeStruct((LANGS, RAN...]
where the time goes in v3:
time: 91 us; the launch traced here: 90.8 us
  Pallas kernels  90 us (99%)
    pallas_call x1, Pallas kernels, on_device(): pl.pallas_call(main_kernel, out_shape=(buf(T, D_ALL), buf(CHIPS, ROWS, G_...  86.7 us
    pallas_call x1, Pallas kernels, on_device(): pl.pallas_call(finish_kernel, out_shape=(jax.ShapeDtypeStruct((LANGS, RAN...  3.32 us

profile of v3, /device:TPU:1, one launch (start us, length us, event | category | flops | bytes accessed | tf_op | source)
XLA Modules:
  0.0 90.8 jit_solution(17435837441179827259)
XLA Ops:
  0.6 86.7 %exchange.1 = (bf16[512,4608]{1,0:T(8,128)(2,1)S(1)}, bf16[8,128,1664]{2,1,0:T(8,128)(2,1)S(1)}) custom-call(s32[512]{0:T(512)} %lang.1, s32[512]{0:T(512)} %live.1, s32[1,512]{1,0:T(1,128)} %bitcast.1, bf16[512,4608]{1,0:T(8,128)(2,1)} %tokens.1, bf16[512,2048]{1,0:T(8,128)(2,1)} %grad.1, bf16[1152,2048]{1,0:T(8,128)(2,1)} %weight.1, ...), custom_call_target="tpu_custom_call" | custom-call | flops 12000000000 | bytes 40000000 | tf_op jit(solution)/shard_map/exchange/pallas_call | solution.py:513
  87.4 3.3 %finish.1 = (bf16[32,32,1152]{2,1,0:T(8,128)(2,1)}, bf16[32,32,512]{2,1,0:T(8,128)(2,1)}, bf16[512,4608]{1,0:T(8,128)(2,1)}) custom-call(bf16[8,128,1664]{2,1,0:T(8,128)(2,1)S(1)} %get-tuple-element.8.gg, bf16[512,4608]{1,0:T(8,128)(2,1)S(1)} %get-tuple-element.9.ig_in), custom_call_target="tpu_custom_call" | custom-call | tf_op jit(solution)/shard_map/finish/pallas_call | solution.py:559

commit v4 on v3

v4 whole, which is shorter than its diff:
```python
import functools

import jax
import jax.numpy as jnp
from jax import lax
from jax.experimental import pallas as pl
from jax.experimental.pallas import tpu as pltpu
from jax.sharding import PartitionSpec as P

MESH = pl.DeviceIdType.MESH
NT = (((1,), (1,)), ((), ()))
NN = (((1,), (0,)), ((), ()))

TILE = 128
TILES = 4
RANK = 32
ROWS = TILES * RANK
LANGS = 32
YN = 4
CHIPS = 8
T = TILE * TILES
D_ALL, Q_ALL = 4608, 2048
D_SH, Q_SH = D_ALL // YN, Q_ALL // YN
G_ALL = D_SH + Q_SH
SUBS = (96, 16)
MAIN = 4 * SUBS[0]
HALF = 4 * sum(SUBS)
TAIL = D_SH - 2 * HALF
MINE = TAIL // 2
LOCAL = 384
SLOTS = (1, 3, 2)
SLOT_OF = {1: 0, 3: 1, 2: 2}
PARTS = ((0, 768), (768, 384), (D_SH, 256), (D_SH + 256, 256))


def dot(a, b, dims=NN):
    return lax.dot_general(a, b, dims, preferred_element_type=jnp.float32)


def one_hot(cond):
    return cond.astype(jnp.float32).astype(jnp.bfloat16)


def iota(shape, dim):
    return lax.broadcasted_iota(jnp.int32, shape, dim)


def permutation(shape):
    i, j = iota(shape, 0), iota(shape, 1)
    k, q, r = lax.div(lax.rem(j, 16), 4), lax.div(j, 16), lax.rem(j, 4)
    return one_hot(i == k * RANK + q * 4 + r)


def main_kernel(
    lang, live, lang_row, tokens, grad, weight, adown, aup,
    ig, gg,
    wbuf, wl, tok, og, adv, auv, su, sd, uu, dd, spd, spu, r1d, r1u, r2d, r2u, xout, xin, gv, b2, btp, htp, pick,
    in_sem, w_s, y_r, a_r, b_r, f_r, c_r, t_r, tf_r, tc_r,
    u_s, u_r, d_s, d_r, pd_s, pd_r, pu_s, pu_r, xd_s, xd_r, xu_s, xu_r, xc_s, xc_r, g_s, g_r, e_s, e_r, own_s,
):
    f, e, o = lax.axis_index("fsdp"), lax.axis_index("dp"), lax.axis_index("owner")
    q, c = lax.div(e, 2), lax.rem(e, 2)
    x, zl = lax.rem(q, 4), lax.div(q, 4)
    z = o * 2 + zl
    pa = (x * (1 - c) + z * c, x)
    pb = (z * (1 - c) + x * c, z)
    swap = (c, 0)

    def mod(v, n):
        return lax.rem(v + n, n)

    def at_ab(t, da, db):
        a, b = mod(pa[t] + da, 4), mod(pb[t] + db, 4)
        xx, zz = a * (1 - swap[t]) + b * swap[t], b * (1 - swap[t]) + a * swap[t]
        return (f, lax.rem(zz, 2) * 8 + xx * 2 + c, lax.div(zz, 2))

    def at_y(s):
        return (mod(f + s, 4), e, o)

    def at_chip(chip):
        return (f, chip * 2 + c, o)

    def chip_of(dz, s):
        return lax.rem(zl + dz, 2) * 4 + mod(x - s, 4)

    other = (f, q * 2 + 1 - c, o)

    def rcopy(src, dst, ssem, rsem, dev):
        return pltpu.make_async_remote_copy(
            src_ref=src, dst_ref=dst, send_sem=ssem, recv_sem=rsem, device_id=dev, device_id_type=MESH
        )

    def await_ref(ref, sem):
        pltpu.make_async_copy(ref, ref, sem).wait()

    def send(*args):
        rcopy(*args).start()

    loads = [
        pltpu.make_async_copy(s, d, in_sem.at[i])
        for i, (s, d) in enumerate(((aup, auv), (adown, adv), (grad, og), (tokens, tok), (weight, wl)))
    ]
    for cp in loads:
        cp.start()

    barrier = pltpu.get_barrier_semaphore()
    peers = [at_y(s) for s in (1, 2, 3)]
    for t in range(2):
        peers += [at_ab(t, s, 0) for s in (1, 2, 3)] + [at_ab(t, 0, 1), at_ab(t, 0, -1)]
    peers += [at_chip(lax.rem(q + s, CHIPS)) for s in range(1, CHIPS)] + [other]
    for dev in peers:
        pl.semaphore_signal(barrier, inc=1, device_id=dev, device_id_type=MESH)
    pl.semaphore_wait(barrier, len(peers))

    def first_row(t, core):
        return core * 4 * SUBS[t] + t * 2 * MAIN

    def piece(ref, slots, t, a, b):
        rows = pl.ds(pl.multiple_of(first_row(t, c) + b * SUBS[t], 16), SUBS[t])
        cols = pl.ds(pl.multiple_of(a * (Q_ALL // 4), TILE), Q_ALL // 4)
        return ref.at[rows, cols] if slots is None else ref.at[slots, rows, cols]

    for s in (1, 3, 2):
        i = SLOT_OF[4 - s]
        for t in range(2):
            send(
                piece(weight, None, t, pa[t], pb[t]), piece(wbuf, i, t, pa[t], pb[t]),
                w_s.at[0], y_r.at[t, i], at_y(s),
            )

    def choose(table, s, out):
        first = ((mod(f + s, 4) * 16 + e) * 2 + o) * TILES
        for k in range(TILES):
            out[pl.ds(k * RANK, RANK), :] = table[lax.rem(lang[first + k], LANGS)]

    loads[2].wait()
    own = ((f * 16 + e) * 2 + o) * TILES
    slot = iota((TILE, Q_ALL), 0)
    for k in range(TILES):
        rows = pl.ds(k * TILE, TILE)
        og[rows, :] = jnp.where(slot < live[own + k], og[rows, :].astype(jnp.float32), 0.0).astype(jnp.bfloat16)

    groups = ((pl.ds(0, 2), (0, 1)), (pl.ds(2, 1), (2,)))
    every = pl.ds(0, 3)

    def b_sends(t, s):
        unit = piece(wbuf, every, t, mod(pa[t] - s, 4), pb[t])
        send(unit, unit, w_s.at[0], b_r.at[t, 0, s], at_ab(t, 0, 1))
        send(unit, unit, w_s.at[0], b_r.at[t, 1, s], at_ab(t, 0, -1))

    for g in range(2):
        for t in range(2):
            for i in groups[g][1]:
                await_ref(piece(wbuf, i, t, pa[t], pb[t]), y_r.at[t, i])
            unit = piece(wbuf, groups[g][0], t, pa[t], pb[t])
            for s in (2, 1, 3):
                send(unit, unit, w_s.at[0], a_r.at[t, s - 1, g], at_ab(t, s, 0))
        if g == 0:
            loads[0].wait()
            for s in (2, 1, 3):
                choose(auv, s, su.at[s - 1])
                send(su.at[s - 1], uu.at[f], u_s.at[0], u_r.at[0], at_y(s))

    choose(auv, 0, uu.at[f])
    n = iota((T, T), 1)
    chip, y, k = lax.div(n, 64), lax.rem(lax.div(n, 16), 4), lax.rem(lax.div(n, 4), 4)
    source = one_hot(iota((T, T), 0) == ((y * 16 + chip * 2 + c) * 2 + o) * TILES + k)
    langs = jnp.broadcast_to(lang_row[...].astype(jnp.float32), (16, T)).astype(jnp.bfloat16)
    langs = dot(langs, source)[:1]
    m, n = iota((ROWS, T), 0), iota((ROWS, T), 1)
    wanted = (lax.div(m, 4) + o * LANGS).astype(jnp.float32)
    pick[...] = one_hot((langs == wanted) & (lax.rem(n, 4) == lax.rem(m, 4)))

    j, t = iota((ROWS, T), 0), iota((ROWS, T), 1)
    limit = jnp.where(
        t < 2 * TILE,
        jnp.where(t < TILE, live[own], live[own + 1]),
        jnp.where(t < 3 * TILE, live[own + 2], live[own + 3]),
    )
    mask = (lax.div(j, RANK) == lax.div(t, TILE)) & (lax.rem(t, TILE) < limit)
    perm_t = permutation((ROWS, ROWS)).astype(jnp.float32).T.astype(jnp.bfloat16)

    def rows_by_chip(v):
        v = jnp.where(mask, v, 0.0).astype(jnp.bfloat16)
        return dot(perm_t, v).astype(jnp.bfloat16)

    await_ref(uu.at[pl.ds(0, 3)], u_r.at[0])
    for t in range(2):
        b_sends(t, 0)
    bt = jnp.zeros((ROWS, T), jnp.float32)
    bb = jnp.zeros((T, ROWS), jnp.float32)
    for y in range(YN):
        bt += dot(uu[y], og[:, y * Q_SH : (y + 1) * Q_SH], NT)
        bb += dot(og[:, y * Q_SH : (y + 1) * Q_SH], uu[y], NT)
    tt, jj = iota((T, ROWS), 0), iota((T, ROWS), 1)
    bb = jnp.where(lax.div(jj, RANK) == lax.div(tt, TILE), bb, 0.0).astype(jnp.bfloat16)
    b2[...] = (bb.astype(jnp.float32) * 2.0).astype(jnp.bfloat16)
    btp[...] = rows_by_chip(bt)

    loads[3].wait()
    for s in (2, 1, 3, 0):
        y = mod(f + s, 4)
        part = dot(btp[...], tok[:, pl.ds(pl.multiple_of(y * D_SH, TILE), D_SH)]).astype(jnp.bfloat16)
        if s:
            spd[s - 1] = part
            send(spd.at[s - 1], r1d.at[f], pd_s.at[0], pd_r.at[0], at_y(s))
        else:
            r1d[f] = part

    loads[1].wait()
    for s in (2, 1, 3):
        choose(adv, s, sd.at[s - 1])
        send(sd.at[s - 1], dd.at[f], d_s.at[0], d_r.at[0], at_y(s))
    choose(adv, 0, dd.at[f])

    def spread(r1, r2, s, ssem, rsem):
        y = mod(f - s, 4)

        def one(i, _):
            chip = lax.rem(q + i, CHIPS)
            rcopy(
                r1.at[y, pl.ds(pl.multiple_of(chip * 16, 16), 16)], r2.at[q, y],
                ssem, rsem, at_chip(chip),
            ).start()
            return 0

        lax.fori_loop(1, CHIPS, one, 0)
        pltpu.make_async_copy(r1.at[y, pl.ds(pl.multiple_of(q * 16, 16), 16)], r2.at[q, y], rsem).start()

    spread(r1d, r2d, 0, xd_s.at[0], xd_r.at[0])

    for s in (1, 3, 2):
        for t in range(2):
            for g in range(2):
                await_ref(piece(wbuf, groups[g][0], t, mod(pa[t] - s, 4), pb[t]), a_r.at[t, s - 1, g])
            b_sends(t, s)

    def block(t, rel):
        rows = pl.ds(pl.multiple_of(first_row(t, c) + mod(pb[t] + rel, 4) * SUBS[t], 16), SUBS[t])
        return wbuf.at[:, rows]

    def block_to_other(t, rel):
        send(block(t, rel), block(t, rel), w_s.at[0], c_r.at[t], other)

    def block_arrived(t):
        await_ref(block(t, 2), f_r.at[t])

    block_to_other(0, 0)

    def way_of(t, s):
        return (1 - swap[t]) * (2 * lax.rem(z, 2) - 1) + swap[t] * (1 if s in (0, 2) else -1)

    def pass_on(t, s):
        way = way_of(t, s)
        unit = piece(wbuf, every, t, mod(pa[t] - s, 4), mod(pb[t] - way, 4))
        await_ref(unit, b_r.at[t, lax.div(1 - way, 2), s])
        send(unit, unit, w_s.at[0], f_r.at[t], at_ab(t, 0, way))

    def rest(t, s):
        way = way_of(t, s)
        await_ref(piece(wbuf, every, t, mod(pa[t] - s, 4), mod(pb[t] + way, 4)), b_r.at[t, lax.div(1 + way, 2), s])

    pass_on(0, 0)

    def columns(w, y, first, width):
        d = dd[y, :, pl.ds(first, width)]
        value = (dot(og[...], w, NT) + dot(b2[...], d)).astype(jnp.bfloat16)
        ig[:, pl.ds(pl.multiple_of(y * D_SH + first, TILE), width)] = value

    loads[4].wait()

    def local_chunk(i, _):
        first = pl.multiple_of(i * LOCAL, TILE)
        columns(wl[pl.ds(first, LOCAL), :], f, first, LOCAL)
        return 0

    lax.fori_loop(0, D_SH // LOCAL, local_chunk, 0)

    def gathered(i, core):
        first = pl.multiple_of(core * MAIN, TILE)
        columns(wbuf[i, pl.ds(first, MAIN), :], mod(f + SLOTS[i], 4), first, MAIN)

    def spread_down(s):
        spread(r1d, r2d, s, xd_s.at[0], xd_r.at[0])

    def spread_up(s):
        spread(r1u, r2u, s, xu_s.at[0], xu_r.at[0])

    await_ref(r1d.at[pl.ds(0, 3)], pd_r.at[0])
    for s in (1, 3, 2):
        spread_down(s)
    for s in (1, 3, 2):
        pass_on(0, s)
    for s in range(4):
        rest(0, s)
    for rel in (1, 3):
        block_to_other(0, rel)
    await_ref(dd.at[pl.ds(0, 3)], d_r.at[0])
    ht = jnp.zeros((ROWS, T), jnp.float32)
    for y in range(YN):
        ht += dot(dd[y], tok[:, y * D_SH : (y + 1) * D_SH], NT)
    htp[...] = rows_by_chip(ht)
    for s in (2, 1, 3, 0):
        y = mod(f + s, 4)
        part = dot(htp[...], og[:, pl.ds(pl.multiple_of(y * Q_SH, TILE), Q_SH)]).astype(jnp.bfloat16)
        if s:
            spu[s - 1] = part
            send(spu.at[s - 1], r1u.at[f], pu_s.at[0], pu_r.at[0], at_y(s))
        else:
            r1u[f] = part
    spread(r1u, r2u, 0, xu_s.at[0], xu_r.at[0])

    def tail_rows(i, late):
        half = (1 - i) * (1 - late) + i * late
        return pl.ds(pl.multiple_of(2 * HALF + c * MINE + half * (MINE // 2), 16), MINE // 2)

    def tail_sends(late):
        for i, s in ((1, 1), (0, 3)):
            rows = tail_rows(i, late)
            send(weight.at[rows], wbuf.at[i, rows], w_s.at[0], t_r.at[i, late], at_y(s))

    tail_sends(0)
    tail_sends(1)

    for s in (0, 1, 3, 2):
        pass_on(1, s)
    block_arrived(0)
    block_to_other(0, 2)

    scale = 2.0 / 256.0

    def send_sum(width):
        part, there = xout.at[:, pl.ds(0, width)], xin.at[:, pl.ds(0, width)]
        return rcopy(part, there, xc_s.at[0], xc_r.at[0], other)

    def place(dz, s, r):
        return gg.at[chip_of(dz, s), :, pl.ds(*PARTS[r])]

    def mine(r):
        return gv.at[:, pl.ds(PARTS[r][0] - (D_SH if r > 1 else 0), PARTS[r][1])]

    def to_x(src, dst, r, k):
        for s in (2, 1, 3):
            rcopy(src, dst, g_s.at[0], g_r.at[r % 2, k + s - 1], at_chip(chip_of(0, -s))).start()

    def to_z(src, dst, r, k):
        rcopy(src, dst, g_s.at[0], g_r.at[r % 2, k], at_chip(chip_of(1, 0))).start()

    def to_core(src, dst, r, k):
        rcopy(src, dst, e_s.at[0], e_r.at[0], other).start()

    def start_gather(r):
        to_z(mine(r + 1), place(0, 0, r + 1), r + 1, 3)
        to_x(mine(r), place(0, 0, r), r, 0)
        to_x(mine(r + 1), place(0, 0, r + 1), r + 1, 0)
        to_z(mine(r), place(0, 0, r), r, 3)
        for h in (r, r + 1):
            to_core(mine(h), place(0, 0, h), h, 0)
            pltpu.make_async_copy(mine(h), place(0, 0, h), own_s.at[0]).start()

    def turn(r):
        part = hand_over(1, 0, r + 1)
        to_x(part, part, r + 1, 4)
        for s in (1, 3, 2):
            part = hand_over(0, s, r)
            to_z(part, part, r, 3 + s)

    def last_hop(r):
        for dz in (0, 1):
            for s in (1, 3, 2):
                hand_over(dz, s, r + 1)
        for s in (0, 1, 3, 2):
            hand_over(1, s, r)

    def hand_over(dz, s, r):
        part = place(dz, s, r)
        await_ref(part, g_r.at[r % 2, s - 1 if dz == 0 else 3 + s])
        to_core(part, part, r, dz * 4 + s)
        return part

    await_ref(r2d, xd_r.at[0])
    down = dot(pick[...], r2d[...].reshape(T, D_SH))

    @pl.when(c == 1)
    def _():
        xout[...] = down
        send_sum(D_SH).start()

    gathered(0, c)
    gathered(1, c)
    await_ref(r1u.at[pl.ds(0, 3)], pu_r.at[0])
    for s in (1, 3, 2):
        spread_up(s)

    @pl.when(c == 0)
    def _():
        await_ref(xin, xc_r.at[0])
        gv[...] = ((down + xin[...]) * scale).astype(jnp.bfloat16)
        start_gather(0)

    gathered(2, c)
    await_ref(r2u, xu_r.at[0])
    up = dot(pick[...], r2u[...].reshape(T, Q_SH))

    @pl.when(c == 0)
    def _():
        xout[:, :Q_SH] = up
        send_sum(Q_SH).start()

    for i, s in ((1, 1), (0, 3)):
        rows = tail_rows(i, 0)
        await_ref(wbuf.at[i, rows], t_r.at[i, 0])
        send(wbuf.at[i, rows], wbuf.at[2, rows], w_s.at[0], tf_r.at[i], at_y(s))

    @pl.when(c == 1)
    def _():
        await_ref(xin.at[:, pl.ds(0, Q_SH)], xc_r.at[0])
        gv[:, :Q_SH] = ((up + xin[:, :Q_SH]) * scale).astype(jnp.bfloat16)
        start_gather(2)

    def from_other(t):
        rows = pl.ds(pl.multiple_of(first_row(t, 1 - c), 16), 4 * SUBS[t])
        await_ref(wbuf.at[:, rows], c_r.at[t])

    from_other(0)
    gathered(0, 1 - c)

    @pl.when(c == 0)
    def _():
        turn(0)

    gathered(1, 1 - c)
    mine_rows = pl.ds(pl.multiple_of(2 * HALF + c * MINE, 16), MINE)
    theirs = pl.ds(pl.multiple_of(2 * HALF + (1 - c) * MINE, 16), MINE)
    for i in range(2):
        await_ref(wbuf.at[i, tail_rows(i, 1)], t_r.at[i, 1])
    near = wbuf.at[pl.ds(0, 2), mine_rows]
    send(near, near, w_s.at[0], tc_r.at[0], other)
    for s in range(4):
        rest(1, s)
    block_arrived(1)
    for rel in range(4):
        block_to_other(1, rel)

    @pl.when(c == 1)
    def _():
        turn(2)

    gathered(2, 1 - c)

    from_other(1)
    await_ref(wbuf.at[pl.ds(0, 2), theirs], tc_r.at[0])
    last = D_SH - 2 * MAIN
    near_sum = dot(og[...], wbuf[0:2, 2 * MAIN :, :].reshape(2 * last, Q_ALL), NT)
    for i in range(2):
        y = mod(f + SLOTS[i], 4)
        value = near_sum[:, i * last : (i + 1) * last] + dot(b2[...], dd[y, :, 2 * MAIN :])
        ig[:, pl.ds(pl.multiple_of(y * D_SH + 2 * MAIN, TILE), last)] = value.astype(jnp.bfloat16)
    for i in range(2):
        await_ref(wbuf.at[2, tail_rows(i, 0)], tf_r.at[i])
    far = wbuf.at[2, mine_rows]
    send(far, far, w_s.at[0], tc_r.at[1], other)

    @pl.when(c == 0)
    def _():
        last_hop(0)

    @pl.when(c == 1)
    def _():
        last_hop(2)

    await_ref(wbuf.at[2, theirs], tc_r.at[1])
    columns(wbuf[2, 2 * MAIN :, :], mod(f + SLOTS[2], 4), 2 * MAIN, last)

    def finish(width, first):
        ours, theirs = pl.ds(first, width), pl.ds(D_SH - first, G_ALL - width)
        await_ref(gg.at[:, :, theirs], e_r.at[0])
        send_sum(G_ALL - width).wait_send()
        await_ref(gv.at[:, pl.ds(0, width)], own_s.at[0])
        await_ref(gg.at[pl.ds(0, CHIPS - 1), :, ours], g_s.at[0])
        await_ref(gg.at[:, :, ours], e_s.at[0])

    @pl.when(c == 0)
    def _():
        finish(D_SH, 0)

    @pl.when(c == 1)
    def _():
        finish(Q_SH, D_SH)

    await_ref(wbuf, w_s.at[0])
    for ref, ssem in ((su, u_s), (sd, d_s), (spd, pd_s), (spu, pu_s)):
        await_ref(ref, ssem.at[0])
    for r1, ssem in ((r1d, xd_s), (r1u, xu_s)):
        await_ref(r1.at[:, pl.ds(0, 16 * (CHIPS - 1))], ssem.at[0])


def finish_kernel(gg, ig_in, down, up, ig, dv, uv, out_s):
    outs = []

    def emit(src, dst, i, g):
        cp = pltpu.make_async_copy(src, dst, out_s.at[i, g])
        cp.start()
        outs.append(cp)

    for g in range(4):
        rows = pl.ds(g * TILE, TILE)
        emit(ig_in.at[rows], ig.at[rows], 2, g)
    perm = permutation((ROWS, ROWS))
    for g in range(4):
        for h in (2 * g, 2 * g + 1):
            rows = gg[:, h * 16 : (h + 1) * 16, :].reshape(ROWS, G_ALL)
            rows = dot(perm, rows).astype(jnp.bfloat16).reshape(4, RANK, G_ALL)
            dv[h * 4 : (h + 1) * 4] = rows[:, :, :D_SH]
            uv[h * 4 : (h + 1) * 4] = rows[:, :, D_SH:]
        part = pl.ds(g * 8, 8)
        emit(dv.at[part], down.at[part], 0, g)
        emit(uv.at[part], up.at[part], 1, g)
    for cp in outs:
        cp.wait()


def on_device(tokens, output_gradient, tile_language, tile_live_count, frozen_weight, adapter_down, adapter_up):
    bf = jnp.bfloat16
    pin = pltpu.with_memory_space_constraint
    tokens, output_gradient, frozen_weight, adapter_down, adapter_up = (
        pin(a, pltpu.HBM) for a in (tokens, output_gradient, frozen_weight, adapter_down, adapter_up)
    )
    hbm, smem, vmem = (pl.BlockSpec(memory_space=s) for s in (pl.ANY, pltpu.SMEM, pltpu.VMEM))
    sem = pltpu.SemaphoreType.DMA

    def sems(*shapes):
        return [sem(s) for s in shapes]

    def buf(*shape, dtype=bf):
        return pltpu.VMEM(shape, dtype)

    ig, gg = pl.pallas_call(
        main_kernel,
        out_shape=(
            buf(T, D_ALL),
            buf(CHIPS, ROWS, G_ALL),
        ),
        in_specs=[smem, smem, vmem, hbm, hbm, hbm, hbm, hbm],
        out_specs=(vmem, vmem),
        scratch_shapes=[
            buf(3, D_SH, Q_ALL),
            buf(D_SH, Q_ALL),
            buf(T, D_ALL),
            buf(T, Q_ALL),
            buf(LANGS, RANK, D_SH),
            buf(LANGS, RANK, Q_SH),
            buf(3, ROWS, Q_SH),
            buf(3, ROWS, D_SH),
            buf(YN, ROWS, Q_SH),
            buf(YN, ROWS, D_SH),
            buf(3, ROWS, D_SH),
            buf(3, ROWS, Q_SH),
            buf(YN, ROWS, D_SH),
            buf(YN, ROWS, Q_SH),
            buf(CHIPS, YN, 16, D_SH),
            buf(CHIPS, YN, 16, Q_SH),
            buf(ROWS, D_SH, dtype=jnp.float32),
            buf(ROWS, D_SH, dtype=jnp.float32),
            buf(ROWS, D_SH),
            buf(T, ROWS),
            buf(ROWS, T),
            buf(ROWS, T),
            buf(ROWS, T),
            *sems((5,), (1,), (2, 3), (2, 3, 2), (2, 2, 4), (2,), (2,), (2, 2), (2,), (2,)),
            *sems(*[(1,)] * 8, *[(1,)] * 4, (1,), (1,), (1,), (2, 7), (1,), (1,), (1,)),
        ],
        compiler_params=pltpu.CompilerParams(
            collective_id=0, has_side_effects=True, vmem_limit_bytes=46 * 2**20
        ),
        cost_estimate=pl.CostEstimate(flops=12 * 10**9, bytes_accessed=40 * 10**6, transcendentals=0),
        name="exchange",
    )(
        pin(tile_language, pltpu.HBM), pin(tile_live_count, pltpu.HBM), tile_language.reshape(1, T),
        tokens, output_gradient, frozen_weight, adapter_down, adapter_up,
    )
    down, up, ig = pl.pallas_call(
        finish_kernel,
        out_shape=(
            jax.ShapeDtypeStruct((LANGS, RANK, D_SH), bf),
            jax.ShapeDtypeStruct((LANGS, RANK, Q_SH), bf),
            jax.ShapeDtypeStruct((T, D_ALL), bf),
        ),
        in_specs=[vmem, vmem],
        out_specs=(hbm, hbm, hbm),
        scratch_shapes=[buf(LANGS, RANK, D_SH), buf(LANGS, RANK, Q_SH), sem((3, 4))],
        compiler_params=pltpu.CompilerParams(vmem_limit_bytes=16 * 2**20),
        name="finish",
    )(pin(gg, pltpu.VMEM), pin(ig, pltpu.VMEM))
    return ig, down, up


def solution(mesh):
    tok = P(("fsdp", "dp", "owner"), None)
    adapter = P("owner", None, "fsdp")
    return jax.shard_map(
        on_device,
        mesh=mesh,
        in_specs=(tok, tok, P(), P(), P("fsdp", None), adapter, adapter),
        out_specs=(tok, adapter, adapter),
        check_vma=False,
    )
```

time: 91 us -> 89.6 us (0.985)
  Pallas kernels: 90 us -> 88.6 us
    pallas_call x1, Pallas kernels: 86.7 us -> 85.3 us  [on_device(): pl.pallas_call(main_kernel, out_shape=(buf(T, D_ALL), buf(CHIPS, ROWS, G_...]
where the time goes in v4:
time: 89.6 us; the launch traced here: 89.4 us
  Pallas kernels  88.6 us (99%)
    pallas_call x1, Pallas kernels, on_device(): pl.pallas_call(main_kernel, out_shape=(buf(T, D_ALL), buf(CHIPS, ROWS, G_...  85.3 us
    pallas_call x1, Pallas kernels, on_device(): pl.pallas_call(finish_kernel, out_shape=(jax.ShapeDtypeStruct((LANGS, RAN...  3.32 us

profile of v4, /device:TPU:1, one launch (start us, length us, event | category | flops | bytes accessed | tf_op | source)
XLA Modules:
  0.0 89.4 jit_solution(14328669913649235957)
XLA Ops:
  0.6 85.3 %exchange.1 = (bf16[512,4608]{1,0:T(8,128)(2,1)S(1)}, bf16[8,128,1664]{2,1,0:T(8,128)(2,1)S(1)}) custom-call(s32[512]{0:T(512)} %lang.1, s32[512]{0:T(512)} %live.1, s32[1,512]{1,0:T(1,128)} %bitcast.1, bf16[512,4608]{1,0:T(8,128)(2,1)} %tokens.1, bf16[512,2048]{1,0:T(8,128)(2,1)} %grad.1, bf16[1152,2048]{1,0:T(8,128)(2,1)} %weight.1, ...), custom_call_target="tpu_custom_call" | custom-call | flops 12000000000 | bytes 40000000 | tf_op jit(solution)/shard_map/exchange/pallas_call | solution.py:538
  85.9 3.3 %finish.1 = (bf16[32,32,1152]{2,1,0:T(8,128)(2,1)}, bf16[32,32,512]{2,1,0:T(8,128)(2,1)}, bf16[512,4608]{1,0:T(8,128)(2,1)}) custom-call(bf16[8,128,1664]{2,1,0:T(8,128)(2,1)S(1)} %get-tuple-element.8.gg, bf16[512,4608]{1,0:T(8,128)(2,1)S(1)} %get-tuple-element.9.ig_in), custom_call_target="tpu_custom_call" | custom-call | tf_op jit(solution)/shard_map/finish/pallas_call | solution.py:582

commit v5 on v4

--- a/solution.py
+++ b/solution.py
@@ -30,7 +30,7 @@
 LOCAL = 384
 SLOTS = (1, 3, 2)
 SLOT_OF = {1: 0, 3: 1, 2: 2}
-PARTS = ((0, 768), (768, 384), (D_SH, 256), (D_SH + 256, 256))
+PARTS = ((0, 640), (640, 512), (D_SH, 256), (D_SH + 256, 256))
 
 
 def dot(a, b, dims=NN):

time: 89.6 us -> 88.5 us (0.988)
  Pallas kernels: 88.6 us -> 87.6 us
    pallas_call x1, Pallas kernels: 85.3 us -> 84.3 us  [on_device(): pl.pallas_call(main_kernel, out_shape=(buf(T, D_ALL), buf(CHIPS, ROWS, G_...]
where the time goes in v5:
time: 88.5 us; the launch traced here: 88.4 us
  Pallas kernels  87.6 us (99%)
    pallas_call x1, Pallas kernels, on_device(): pl.pallas_call(main_kernel, out_shape=(buf(T, D_ALL), buf(CHIPS, ROWS, G_...  84.3 us
    pallas_call x1, Pallas kernels, on_device(): pl.pallas_call(finish_kernel, out_shape=(jax.ShapeDtypeStruct((LANGS, RAN...  3.32 us

profile of v5, /device:TPU:1, one launch (start us, length us, event | category | flops | bytes accessed | tf_op | source)
XLA Modules:
  0.0 88.4 jit_solution(2991080230281318193)
XLA Ops:
  0.6 84.3 %exchange.1 = (bf16[512,4608]{1,0:T(8,128)(2,1)S(1)}, bf16[8,128,1664]{2,1,0:T(8,128)(2,1)S(1)}) custom-call(s32[512]{0:T(512)} %lang.1, s32[512]{0:T(512)} %live.1, s32[1,512]{1,0:T(1,128)} %bitcast.1, bf16[512,4608]{1,0:T(8,128)(2,1)} %tokens.1, bf16[512,2048]{1,0:T(8,128)(2,1)} %grad.1, bf16[1152,2048]{1,0:T(8,128)(2,1)} %weight.1, ...), custom_call_target="tpu_custom_call" | custom-call | flops 12000000000 | bytes 40000000 | tf_op jit(solution)/shard_map/exchange/pallas_call | solution.py:538
  84.9 3.3 %finish.1 = (bf16[32,32,1152]{2,1,0:T(8,128)(2,1)}, bf16[32,32,512]{2,1,0:T(8,128)(2,1)}, bf16[512,4608]{1,0:T(8,128)(2,1)}) custom-call(bf16[8,128,1664]{2,1,0:T(8,128)(2,1)S(1)} %get-tuple-element.8.gg, bf16[512,4608]{1,0:T(8,128)(2,1)S(1)} %get-tuple-element.9.ig_in), custom_call_target="tpu_custom_call" | custom-call | tf_op jit(solution)/shard_map/finish/pallas_call | solution.py:582

commit v6 on v5

--- a/solution.py
+++ b/solution.py
@@ -159,7 +159,7 @@
             loads[0].wait()
             for s in (2, 1, 3):
                 choose(auv, s, su.at[s - 1])
-                send(su.at[s - 1], uu.at[f], u_s.at[0], u_r.at[0], at_y(s))
+                send(su.at[s - 1], uu.at[f], u_s.at[0], u_r.at[s - 1], at_y(s))
 
     choose(auv, 0, uu.at[f])
     n = iota((T, T), 1)
@@ -184,14 +184,17 @@
         v = jnp.where(mask, v, 0.0).astype(jnp.bfloat16)
         return dot(perm_t, v).astype(jnp.bfloat16)
 
-    await_ref(uu.at[pl.ds(0, 3)], u_r.at[0])
     for t in range(2):
         b_sends(t, 0)
     bt = jnp.zeros((ROWS, T), jnp.float32)
     bb = jnp.zeros((T, ROWS), jnp.float32)
-    for y in range(YN):
-        bt += dot(uu[y], og[:, y * Q_SH : (y + 1) * Q_SH], NT)
-        bb += dot(og[:, y * Q_SH : (y + 1) * Q_SH], uu[y], NT)
+    for s in (0, 1, 3, 2):
+        y = mod(f - s, 4)
+        if s:
+            await_ref(uu.at[y], u_r.at[s - 1])
+        rows = og[:, pl.ds(pl.multiple_of(y * Q_SH, TILE), Q_SH)]
+        bt += dot(uu[y], rows, NT)
+        bb += dot(rows, uu[y], NT)
     tt, jj = iota((T, ROWS), 0), iota((T, ROWS), 1)
     bb = jnp.where(lax.div(jj, RANK) == lax.div(tt, TILE), bb, 0.0).astype(jnp.bfloat16)
     b2[...] = (bb.astype(jnp.float32) * 2.0).astype(jnp.bfloat16)
@@ -210,7 +213,7 @@
     loads[1].wait()
     for s in (2, 1, 3):
         choose(adv, s, sd.at[s - 1])
-        send(sd.at[s - 1], dd.at[f], d_s.at[0], d_r.at[0], at_y(s))
+        send(sd.at[s - 1], dd.at[f], d_s.at[0], d_r.at[s - 1], at_y(s))
     choose(adv, 0, dd.at[f])
 
     def spread(r1, r2, s, ssem, rsem):
@@ -295,10 +298,12 @@
         rest(0, s)
     for rel in (1, 3):
         block_to_other(0, rel)
-    await_ref(dd.at[pl.ds(0, 3)], d_r.at[0])
     ht = jnp.zeros((ROWS, T), jnp.float32)
-    for y in range(YN):
-        ht += dot(dd[y], tok[:, y * D_SH : (y + 1) * D_SH], NT)
+    for s in (0, 1, 3, 2):
+        y = mod(f - s, 4)
+        if s:
+            await_ref(dd.at[y], d_r.at[s - 1])
+        ht += dot(dd[y], tok[:, pl.ds(pl.multiple_of(y * D_SH, TILE), D_SH)], NT)
     htp[...] = rows_by_chip(ht)
     for s in (2, 1, 3, 0):
         y = mod(f + s, 4)
@@ -568,7 +573,7 @@
             buf(ROWS, T),
             buf(ROWS, T),
             *sems((5,), (1,), (2, 3), (2, 3, 2), (2, 2, 4), (2,), (2,), (2, 2), (2,), (2,)),
-            *sems(*[(1,)] * 8, *[(1,)] * 4, (1,), (1,), (1,), (2, 7), (1,), (1,), (1,)),
+            *sems((1,), (3,), (1,), (3,), *[(1,)] * 4, *[(1,)] * 4, (1,), (1,), (1,), (2, 7), (1,), (1,), (1,)),
         ],
         compiler_params=pltpu.CompilerParams(
             collective_id=0, has_side_effects=True, vmem_limit_bytes=46 * 2**20

time: 88.5 us -> 87.8 us (level)
  no operation moved by 1% of the time
where the time goes in v6:
time: 87.8 us; the launch traced here: 87.6 us
  Pallas kernels  86.8 us (99%)
    pallas_call x1, Pallas kernels, on_device(): pl.pallas_call(main_kernel, out_shape=(buf(T, D_ALL), buf(CHIPS, ROWS, G_...  83.5 us
    pallas_call x1, Pallas kernels, on_device(): pl.pallas_call(finish_kernel, out_shape=(jax.ShapeDtypeStruct((LANGS, RAN...  3.32 us

profile of v6, /device:TPU:1, one launch (start us, length us, event | category | flops | bytes accessed | tf_op | source)
XLA Modules:
  0.0 87.6 jit_solution(17776970207231491323)
XLA Ops:
  0.6 83.5 %exchange.1 = (bf16[512,4608]{1,0:T(8,128)(2,1)S(1)}, bf16[8,128,1664]{2,1,0:T(8,128)(2,1)S(1)}) custom-call(s32[512]{0:T(512)} %lang.1, s32[512]{0:T(512)} %live.1, s32[1,512]{1,0:T(1,128)} %bitcast.1, bf16[512,4608]{1,0:T(8,128)(2,1)} %tokens.1, bf16[512,2048]{1,0:T(8,128)(2,1)} %grad.1, bf16[1152,2048]{1,0:T(8,128)(2,1)} %weight.1, ...), custom_call_target="tpu_custom_call" | custom-call | flops 12000000000 | bytes 40000000 | tf_op jit(solution)/shard_map/exchange/pallas_call | solution.py:543
  84.2 3.3 %finish.1 = (bf16[32,32,1152]{2,1,0:T(8,128)(2,1)}, bf16[32,32,512]{2,1,0:T(8,128)(2,1)}, bf16[512,4608]{1,0:T(8,128)(2,1)}) custom-call(bf16[8,128,1664]{2,1,0:T(8,128)(2,1)S(1)} %get-tuple-element.8.gg, bf16[512,4608]{1,0:T(8,128)(2,1)S(1)} %get-tuple-element.9.ig_in), custom_call_target="tpu_custom_call" | custom-call | tf_op jit(solution)/shard_map/finish/pallas_call | solution.py:587
